TPU v7x, 32 devices: a whole 2x2x4 slice. The times are simulated.
32 devices in a mesh: row: 4 (over z), col: 8 (over y, x, core).
Axes of the slice: x: 2, y: 2, z: 4, core: 2. Of those that a mesh axis runs over, the one named last changes fastest.
Arguments:
- matrix: float32 [4, 4, 256, 2, 8, 256], P(None, 'row', None, None, 'col'), may hold values from -6 to 6
- panel_t: float32 [256, 4, 4, 256], P('col', None, 'row'), may hold values from -3 to 3
Outputs:
- updated: float32 [4, 4, 256, 2, 8, 256], P(None, 'row', None, None, 'col')
- vectors: float32 [256, 4, 4, 256], P('col', None, 'row')
- band_block: float32 [256, 256], replicated
- reflector_factor: float32 [256, 256], replicated
All inputs are finite; a program needn't handle non-finite values.
Results may differ from a plain program's by a relative error of at most 0.00017.
Values sent between devices are 32-bit elements; how exact they have to be, the bound alone decides.
A program may use at most 64 MiB of HBM per device.

v0:
```python
import jax
import jax.numpy as jnp
from jax import lax
from jax.sharding import PartitionSpec as P


def from_root(value, axis, source):
    kept = jnp.where(lax.axis_index(axis) == source, value, 0).astype(value.dtype)
    return lax.psum(kept, axis)


def matmul(multiplier, multiplicand):
    return jnp.dot(multiplier, multiplicand, precision=lax.Precision.HIGHEST)


def contract_first(multiplier, multiplicand):
    return lax.dot_general(
        multiplier, multiplicand, (((0,), (0,)), ((), ())), precision=lax.Precision.HIGHEST
    )


def contract_last(multiplier, multiplicand):
    return lax.dot_general(
        multiplier, multiplicand, (((1,), (1,)), ((), ())), precision=lax.Precision.HIGHEST
    )


def lower_solve(factor, right_side, transposed):
    return lax.linalg.triangular_solve(
        factor, right_side, left_side=True, lower=True, transpose_a=transposed
    )


def pick_slots(block_t, tile_cols, groups, slot_index):
    leading = block_t.shape[0]
    shaped = block_t.reshape(leading, tile_cols, groups, block_t.shape[1] // (tile_cols * groups))
    picked = lax.dynamic_index_in_dim(shaped, slot_index, 2, keepdims=False)
    return picked.reshape(leading, -1)


def body(matrix, panel_t):
    tile_rows = matrix.shape[0]
    tile_size = matrix.shape[2]
    tile_cols = matrix.shape[3]
    row_count = lax.axis_size("row")
    col_count = lax.axis_size("col")
    row_index = lax.axis_index("row")
    col_index = lax.axis_index("col")
    groups = col_count // row_count
    slot_index = col_index // row_count
    root_row = col_index % row_count
    local_rows = tile_rows * tile_size
    local_cols = tile_cols * tile_size
    stored = matrix.reshape(local_rows, local_cols)
    identity = jnp.eye(tile_size, dtype=jnp.float32)
    gathered = lax.all_gather(panel_t, "col", axis=0, tiled=True)
    panel_rows_t = gathered.reshape(tile_size, local_rows)
    first_gram = lax.psum(matmul(panel_rows_t, panel_rows_t.T), "row")
    first_factor = jnp.linalg.cholesky(first_gram)
    orthonormal = lower_solve(first_factor, panel_rows_t, False)
    band_block = -first_factor.T
    top_flag = (row_index == 0).astype(jnp.float32)
    vectors_t = jnp.concatenate(
        [orthonormal[:, :tile_size] + top_flag * identity, orthonormal[:, tile_size:]], axis=1
    )
    top_block = from_root(orthonormal[:, :tile_size], "row", 0) + identity
    top_factor = jnp.linalg.cholesky(contract_first(top_block, top_block))
    reflector = lower_solve(top_factor, lower_solve(top_factor, top_block.T, False), True)
    vectors_c = from_root(pick_slots(vectors_t, tile_cols, groups, slot_index), "row", root_row)
    row_numbers = jnp.arange(local_rows)
    col_numbers = jnp.arange(local_cols)
    global_row = (
        row_numbers // tile_size * row_count + row_index
    ) * tile_size + row_numbers % tile_size
    global_col = (
        col_numbers // tile_size * col_count + col_index
    ) * tile_size + col_numbers % tile_size
    on_lower = global_row[:, None] >= global_col[None, :]
    lower_part = jnp.where(on_lower, stored, 0.0)
    strict_part = jnp.where(global_row[:, None] > global_col[None, :], stored, 0.0)
    row_terms = contract_last(vectors_c, lower_part)
    mirror_terms = matmul(vectors_t, strict_part)
    column_sums = lax.psum(mirror_terms, "row")
    wanted = ((jnp.arange(groups) == slot_index) & (root_row == row_index)).astype(jnp.float32)
    spread = column_sums.reshape(tile_size, tile_cols, 1, tile_size) * wanted[None, None, :, None]
    products_t = lax.psum(row_terms + spread.reshape(tile_size, local_rows), "col")
    curvature = lax.psum(contract_last(vectors_t, products_t), "row")
    mixed_term = matmul(matmul(reflector.T, curvature), reflector)
    update_rows_t = matmul(reflector.T, products_t) - 0.5 * matmul(mixed_term.T, vectors_t)
    update_cols_t = from_root(
        pick_slots(update_rows_t, tile_cols, groups, slot_index), "row", root_row
    )
    correction = contract_first(vectors_t, update_cols_t) + contract_first(update_rows_t, vectors_c)
    updated = jnp.where(on_lower, stored - correction, 0.0).reshape(matrix.shape)
    vector_rows = tile_size // col_count
    vectors_out = lax.dynamic_slice_in_dim(
        vectors_t, col_index * vector_rows, vector_rows, 0
    ).reshape(panel_t.shape)
    return (updated, vectors_out, band_block, reflector)


def solution(mesh):
    placed = (P(None, "row", None, None, "col", None), P("col", None, "row", None))
    return jax.shard_map(
        body,
        mesh=mesh,
        in_specs=placed,
        out_specs=(P(None, "row", None, None, "col", None), P("col", None, "row", None), P(), P()),
        check_vma=False,
    )
```

profile of v0, /device:TPU:0, one launch (start us, length us, event | category | flops | bytes accessed | tf_op | source)
XLA Modules:
  0.0 459.0 jit_solution(18369998353622196225)
XLA Ops:
  7.2 1.6 copy.12
  8.9 9.0 %reduce.8 = f32[4,256,2,256]{3,2,1,0:T(2,128)} reduce(f32[4,1,256,2,1,256]{5,4,3,2,1,0:T(1,128)} %param.3, f32[]{:T(128)} %constant.202), dimensions={1,4}, to_apply=%param.3.reduce_sub_computation | reduce | bytes 4194308 | tf_op args[0]
  17.9 1.8 copy.22
  20.2 16.5 %all-gather.2.cloned.1.call-done = f32[256,4,1,256]{3,0,1,2:T(8,128)} async-done(((f32[32,4,1,256]{3,0,1,2:T(8,128)}), f32[256,4,1,256]{3,0,1,2:T(8,128)}) %all-gather.2.cloned.1.call-update) | async-done | bytes 1048592 | tf_op jit(solution)/shard_map/all_gather | solution.py:56
  36.7 3.4 convolution_bitcast_fusion
  41.4 1.2 copy.15
  42.6 1.2 copy.16
  43.9 31.7 %all-reduce.9.cloned.1.call-done = f32[256,256]{0,1:T(8,128)} async-done(((f32[256,256]{0,1:T(8,128)}), f32[256,256]{0,1:T(8,128)}) %all-reduce.9.cloned.1.call-update) | async-done | bytes 262160 | tf_op jit(solution)/shard_map/psum | solution.py:58
  75.6 1.1 copy.14
  78.3 11.7 %cholesky.130 = f32[128,128]{1,0:T(8,128)S(1)} custom-call(f32[128,128]{1,0:T(8,128)S(1)} %cholesky.194), custom_call_target="Cholesky" | custom-call | tf_op jit(solution)/shard_map/jit(cholesky)/cholesky | solution.py:59
  90.1 9.8 %custom-call.19 = f32[1,128,128]{1,2,0:T(8,128)S(1)} custom-call(f32[1,128,128]{2,1,0:T(8,128)S(1)} %get-tuple-element.66), custom_call_target="InvertDiagBlocksLowerTriangular" | custom-call | tf_op jit(solution)/shard_map/jit(cholesky)/cholesky | solution.py:59
  101.0 1.1 convolution_subtract_fusion.4
  102.1 11.7 %cholesky.147 = f32[128,128]{1,0:T(8,128)S(1)} custom-call(f32[128,128]{1,0:T(8,128)S(1)} %convolution_subtract_fusion.4), custom_call_target="Cholesky" | custom-call | tf_op jit(solution)/shard_map/jit(cholesky)/cholesky | solution.py:59
  115.8 1.7 negate_bitcast_fusion
  118.2 4.4 while.2
  119.2 1.4 bitcast_dynamic-update-slice_fusion.4
  121.2 1.4 bitcast_dynamic-update-slice_fusion.4
  123.3 20.5 %custom-call.16 = f32[2,128,128]{1,2,0:T(8,128)S(1)} custom-call(f32[2,128,128]{2,1,0:T(8,128)} %copy-done.12), custom_call_target="InvertDiagBlocksLowerTriangular" | custom-call | tf_op jit(solution)/shard_map/triangular_solve | solution.py:29
  146.9 1.9 reshape.124
  148.8 3.0 fusion.1
  151.8 2.1 mul.78
  153.9 3.1 fusion.14
  158.0 51.9 %all-reduce.17.cloned.1.call-done = (f32[256,512]{1,0:T(8,128)}, f32[256,2,256]{2,1,0:T(2,128)}) async-done(((f32[256,512]{1,0:T(8,128)}, f32[256,2,256]{2,1,0:T(2,128)}), (f32[256,512]{1,0:T(8,128)}, f32[256,2,256]{2,1,0:T(2,128)})) %all-reduce.17.cloned.1.call-update) | async-done | bytes 1048592 | tf_op jit(solution)/shard_map/psum | solution.py:9
  209.9 2.4 mul.79
  212.3 3.0 mul.80
  215.3 4.4 fusion.4
  219.8 56.1 %all-reduce.11.cloned.1.call-done = f32[256,1024]{1,0:T(8,128)} async-done(((f32[256,1024]{1,0:T(8,128)}), f32[256,1024]{1,0:T(8,128)}) %all-reduce.11.cloned.1.call-update) | async-done | bytes 1048592 | tf_op jit(solution)/shard_map/psum | solution.py:86
  275.9 3.0 fusion.65
  279.1 37.5 %all-reduce.15.cloned.1.call-done = (f32[256,256]{1,0:T(8,128)}, f32[256,256]{1,0:T(8,128)}) async-done(((f32[256,256]{1,0:T(8,128)}, f32[256,256]{1,0:T(8,128)}), (f32[256,256]{1,0:T(8,128)}, f32[256,256]{1,0:T(8,128)})) %all-reduce.15.cloned.1.call-update) | async-done | bytes 524304 | tf_op jit(solution)/shard_map/psum | solution.py:9
  316.6 1.6 fusion.20
  318.2 1.7 fusion.19
  322.5 11.7 %cholesky.164 = f32[128,128]{1,0:T(8,128)S(1)} custom-call(f32[128,128]{1,0:T(8,128)S(1)} %cholesky.197), custom_call_target="Cholesky" | custom-call | tf_op jit(solution)/shard_map/jit(cholesky)/cholesky | solution.py:67
  334.2 9.8 %custom-call.20 = f32[1,128,128]{1,2,0:T(8,128)S(1)} custom-call(f32[1,128,128]{2,1,0:T(8,128)S(1)} %get-tuple-element.62), custom_call_target="InvertDiagBlocksLowerTriangular" | custom-call | tf_op jit(solution)/shard_map/jit(cholesky)/cholesky | solution.py:67
  345.1 1.1 convolution_subtract_fusion.3
  346.2 11.7 %cholesky.181 = f32[128,128]{1,0:T(8,128)S(1)} custom-call(f32[128,128]{1,0:T(8,128)S(1)} %convolution_subtract_fusion.3), custom_call_target="Cholesky" | custom-call | tf_op jit(solution)/shard_map/jit(cholesky)/cholesky | solution.py:67
  361.7 4.1 while.3
  362.3 1.4 bitcast_dynamic-update-slice_fusion.5
  364.4 1.4 bitcast_dynamic-update-slice_fusion.5
  366.5 20.7 %custom-call.17 = f32[2,128,128]{1,2,0:T(8,128)S(1)} custom-call(f32[2,128,128]{2,1,0:T(8,128)} %copy-done.11), custom_call_target="InvertDiagBlocksLowerTriangular" | custom-call | tf_op jit(solution)/shard_map/triangular_solve | solution.py:29
  387.2 1.3 fusion.21
  388.5 1.3 convolution_subtract_fusion.2
  393.1 2.0 fusion.5
  395.1 3.1 reshape.125
  398.2 3.1 fusion.15
  403.8 36.7 %all-reduce.13.cloned.1.call-done = f32[256,512]{1,0:T(8,128)} async-done(((f32[256,512]{1,0:T(8,128)}), f32[256,512]{1,0:T(8,128)}) %all-reduce.13.cloned.1.call-update) | async-done | bytes 524304 | tf_op jit(solution)/shard_map/psum | solution.py:9
  440.5 3.0 fusion.68
  443.5 3.7 compare_select_fusion
  447.2 4.7 %reshape.167 = f32[4,1,256,2,1,256]{5,4,3,2,1,0:T(1,128)} reshape(f32[1024,512]{1,0:T(8,128)} %compare_select_fusion) | data formatting | bytes 4194304 | tf_op jit(solution)/shard_map/reshape | solution.py:94
  (92 shorter events, 25.9 us)
Async XLA Ops:
  7.2 29.5 %all-gather.2.cloned.1.call-start = ((), (), s32[]{:S(2)}) async-start(), calls=%async_computation | async-start | bytes 1179648 | tf_op jit(solution)/shard_map/all_gather | solution.py:56
  8.8 66.7 %all-reduce.9.cloned.1.call-start = ((), (), s32[]{:S(2)}) async-start(), calls=%async_computation.1 | async-start | bytes 524288 | tf_op jit(solution)/shard_map/psum | solution.py:58
  36.7 3.6 copy-start.2
  40.1 169.8 %all-reduce.17.cloned.1.call-start = ((), (), s32[]{:S(2)}) async-start(), calls=%async_computation.5 | async-start | bytes 2097152 | tf_op jit(solution)/shard_map/psum | solution.py:9
  77.6 0.7 copy-start.8
  113.9 1.9 copy-start.6
  122.6 0.7 copy-start.12
  157.8 118.1 %all-reduce.11.cloned.1.call-start = ((), (), s32[]{:S(2)}) async-start(), calls=%async_computation.2 | async-start | bytes 2097152 | tf_op jit(solution)/shard_map/psum | solution.py:86
  219.8 96.8 %all-reduce.15.cloned.1.call-start = ((), (), s32[]{:S(2)}) async-start(), calls=%async_computation.4 | async-start | bytes 1048576 | tf_op jit(solution)/shard_map/psum | solution.py:9
  278.9 161.6 %all-reduce.13.cloned.1.call-start = ((), (), s32[]{:S(2)}) async-start(), calls=%async_computation.3 | async-start | bytes 1048576 | tf_op jit(solution)/shard_map/psum | solution.py:9
  321.7 0.7 copy-start.9
  358.0 2.7 copy-start.5
  365.8 0.7 copy-start.11
  387.2 3.9 copy-start.10
  387.2 4.9 %copy-start.3 = (f32[256,1024]{1,0:T(8,128)S(1)}, f32[256,1024]{1,0:T(8,128)}, u32[]{:S(2)}) copy-start(f32[256,1024]{1,0:T(8,128)} %all-reduce.11.cloned.1.call-done) | copy-start | bytes 3145732
  391.0 4.1 copy-start.1
  398.2 4.8 %copy-start.7 = (f32[256,256]{0,1:T(8,128)S(1)}, f32[256,256]{0,1:T(8,128)}, u32[]{:S(2)}) copy-start(f32[256,256]{0,1:T(8,128)} %get-tuple-element.57) | copy-start | bytes 786436
  440.5 3.0 copy-start
  440.5 3.0 copy-start.4
Sparse Core Ops, SparseCore 0:
  10.5 26.1 all-gather.1
  40.2 35.3 all-reduce.8
  157.9 51.9 all-reduce.16
  219.9 55.9 all-reduce.10
  279.0 37.5 all-reduce.14
  402.2 38.2 all-reduce.12
where the time goes:
time: 466 us; the launch traced here: 459 us
  waiting for transfers between devices  230 us (49%)
  other arithmetic  133 us (29%)
  local copies, waits for them, and re-layouts  40.9 us (9%)
  matrix products  36.4 us (8%)
  between operations  17.4 us (4%)
    psum x3, waiting for transfers between devices, from_root(): return lax.psum(kept, axis)  126 us
    psum x1, waiting for transfers between devices, body(): lax.psum(row_terms + spread.reshape(tile_size, local_rows), 'col')  56.1 us
    another operation x5, other arithmetic, lower_solve(): lax.linalg.triangular_solve(factor, right_side, left_side=True, lower=Tru...  42.7 us
    another operation x7, other arithmetic, body(): top_factor = jnp.linalg.cholesky(contract_first(top_block, top_block))  34.7 us
    another operation x6, other arithmetic, body(): first_factor = jnp.linalg.cholesky(first_gram)  33.9 us
    psum x1, waiting for transfers between devices, body(): first_gram = lax.psum(matmul(panel_rows_t, panel_rows_t.T), 'row')  31.7 us
    all_gather x1, waiting for transfers between devices, body(): gathered = lax.all_gather(panel_t, 'col', axis=0, tiled=True)  16.5 us
    dot_general x6, matrix products, matmul(): return jnp.dot(multiplier, multiplicand, precision=lax.Precision.HIGHEST)  10.3 us
  transfers between devices with their start and end apart: 6, of which 6 were waited for; matrix products, arithmetic and copies ran while one was open for 4% of the time, Pallas kernels for 0%

commit v1 on v0

v1 whole, which is shorter than its diff:
```python
import functools

import jax
import jax.numpy as jnp
from jax import lax
from jax.experimental import pallas as pl
from jax.experimental.pallas import tpu as pltpu
from jax.sharding import PartitionSpec as P

F32 = jnp.float32
VMEM = pltpu.VMEM
HIGHEST = lax.Precision.HIGHEST
HIGH = lax.Precision.HIGH
BLOCK = 64
GROUP = 4


def dot(a, b, over, precision=HIGHEST):
    return lax.dot_general(a, b, (over, ((), ())), precision=precision, preferred_element_type=F32)


NN = ((1,), (0,))
TN = ((0,), (0,))
NT = ((1,), (1,))


def in_vmem(count):
    return [pl.BlockSpec(memory_space=VMEM)] * count


def params(collective=None):
    if collective is None:
        return pltpu.CompilerParams(vmem_limit_bytes=48 << 20)
    return pltpu.CompilerParams(
        vmem_limit_bytes=48 << 20, collective_id=collective, has_side_effects=True
    )


def shape(*dims):
    return jax.ShapeDtypeStruct(dims, F32)


def inverse_factor(block):
    size = block.shape[0]
    row = lax.broadcasted_iota(jnp.int32, (size, 2 * size), 0)
    col = lax.broadcasted_iota(jnp.int32, (size, 2 * size), 1)
    work = jnp.concatenate([block, jnp.zeros_like(block)], axis=1)
    work = jnp.where(col == row + size, 1.0, work)
    scale = jnp.zeros((size, 2 * size), F32)
    for first in range(0, size, GROUP):
        cols = [
            jnp.broadcast_to(work[:, first + t : first + t + 1], (size, 2 * size))
            for t in range(GROUP)
        ]
        for t in range(GROUP):
            j = first + t
            pivot = cols[t][j : j + 1, :]
            factor = jnp.where(row > j, cols[t] * (1.0 / pivot), 0.0)
            for u in range(t + 1, GROUP):
                cols[u] = cols[u] - factor * cols[u][j : j + 1, :]
            work = work - factor * work[j : j + 1, :]
            scale = jnp.where(row == j, lax.rsqrt(pivot), scale)
    return (work * scale)[:, size:]


def factor_into(gram, work, upper_ref, inverse_ref):
    size = gram.shape[0]
    ident = (
        lax.broadcasted_iota(jnp.int32, (size, size), 0)
        == lax.broadcasted_iota(jnp.int32, (size, size), 1)
    ).astype(F32)
    work[:, :size] = gram
    work[:, size:] = ident
    for lo in range(0, size, BLOCK):
        hi = lo + BLOCK
        inv = inverse_factor(work[lo:hi, lo:hi])
        rows = dot(inv, work[lo:hi, :], NN)
        work[lo:hi, :] = rows
        if hi < size:
            work[hi:, :] -= dot(rows[:, hi:size], rows, TN)
    upper = work[:, :size]
    keep = lax.broadcasted_iota(jnp.int32, (size, size), 1) >= lax.broadcasted_iota(
        jnp.int32, (size, size), 0
    )
    upper_ref[...] = jnp.where(keep, upper, 0.0)
    inverse_ref[...] = work[:, size:]


def panel_kernel(gram_ref, top_ref, band_ref, inverse_ref, reflector_ref, work, upper):
    size = gram_ref.shape[0]
    ident = (
        lax.broadcasted_iota(jnp.int32, (size, size), 0)
        == lax.broadcasted_iota(jnp.int32, (size, size), 1)
    ).astype(F32)
    factor_into(gram_ref[...], work, upper, inverse_ref)
    band_ref[...] = -upper[...]
    block = dot(inverse_ref[...], top_ref[...], NN) + ident
    factor_into(dot(block, block, TN), work, upper, reflector_ref)
    inv = reflector_ref[...]
    reflector_ref[...] = dot(inv, dot(inv, block, NT), TN)


def panel_factors(gram, top):
    size = gram.shape[0]
    return pl.pallas_call(
        panel_kernel,
        out_shape=[shape(size, size)] * 3,
        in_specs=in_vmem(2),
        out_specs=in_vmem(3),
        scratch_shapes=[VMEM((size, 2 * size), F32), VMEM((size, size), F32)],
        compiler_params=params(),
    )(gram, top)


def greet(row_peers, col_peers):
    barrier = pltpu.get_barrier_semaphore()
    for peer in row_peers:
        pl.semaphore_signal(
            barrier, inc=1, device_id={"row": peer}, device_id_type=pl.DeviceIdType.MESH
        )
    for peer in col_peers:
        pl.semaphore_signal(
            barrier, inc=1, device_id={"col": peer}, device_id_type=pl.DeviceIdType.MESH
        )
    pl.semaphore_wait(barrier, len(row_peers) + len(col_peers))


def copy_to(axis, peer, src, dst, send, recv):
    return pltpu.make_async_remote_copy(
        src_ref=src,
        dst_ref=dst,
        send_sem=send,
        recv_sem=recv,
        device_id={axis: peer},
        device_id_type=pl.DeviceIdType.MESH,
    )


def others(me, count, step=1):
    return [lax.rem(me + k, count) for k in range(step, count, step)]


def sibling_of(me):
    return me + 1 - 2 * lax.rem(me, 2)


def col_gather(src, out, near_send, near_recv, far_send, far_recv, count):
    me = lax.axis_index("col")
    sibling = sibling_of(me)
    started = []
    for k, peer in enumerate(others(me, count, 2)):
        copy = copy_to("col", peer, src, out.at[me], far_send.at[k], far_recv.at[me])
        copy.start()
        started.append(copy)
    copy = copy_to("col", sibling, src, out.at[me], near_send.at[me], near_recv.at[me])
    copy.start()
    started.append(copy)
    out[me] = src[...]
    for peer in others(me, count, 2):
        copy_to("col", peer, src, out.at[peer], far_send.at[0], far_recv.at[peer]).wait_recv()
        copy = copy_to(
            "col", sibling, out.at[peer], out.at[peer], near_send.at[peer], near_recv.at[peer]
        )
        copy.start()
        started.append(copy)
    for k in range(0, count, 2):
        slot = lax.rem(sibling + k, count)
        copy_to(
            "col", sibling, src, out.at[slot], near_send.at[slot], near_recv.at[slot]
        ).wait_recv()
    return started


def gather_sems(count):
    return [
        pltpu.SemaphoreType.DMA((count,)),
        pltpu.SemaphoreType.DMA((count,)),
        pltpu.SemaphoreType.DMA((count // 2,)),
        pltpu.SemaphoreType.DMA((count,)),
    ]


def gather_kernel(count, src, out, *sems):
    me = lax.axis_index("col")
    greet([], others(me, count, 2) + [sibling_of(me)])
    for copy in col_gather(src, out, *sems, count):
        copy.wait_send()


def gather_panel(block, count):
    return pl.pallas_call(
        functools.partial(gather_kernel, count),
        out_shape=shape(count, *block.shape),
        in_specs=in_vmem(1),
        out_specs=in_vmem(1)[0],
        scratch_shapes=gather_sems(count),
        compiler_params=params(0),
    )(block)


def root_send(value, row_count, root, me, out, send, recv):
    @pl.when(me == root)
    def _():
        for k in range(1, row_count):
            copy_to(
                "row", lax.rem(root + k, row_count), value, out, send.at[k - 1], recv
            ).start()


def root_wait(value, row_count, root, me, out, send, recv):
    @pl.when(me == root)
    def _():
        for k in range(1, row_count):
            copy_to(
                "row", lax.rem(root + k, row_count), value, out, send.at[k - 1], recv
            ).wait_send()
        out[...] = value[...]

    @pl.when(me != root)
    def _():
        copy_to("row", root, value, out, send.at[0], recv).wait_recv()


def row_sum(src, slots, send, recv, row_count):
    me = lax.axis_index("row")
    started = []
    for k, peer in enumerate(others(me, row_count)):
        copy = copy_to("row", peer, src, slots.at[me], send.at[k], recv.at[me])
        copy.start()
        started.append(copy)
    slots[me] = src[...]
    for peer in others(me, row_count):
        copy_to("row", peer, src, slots.at[peer], send.at[0], recv.at[peer]).wait_recv()
    total = slots[0]
    for k in range(1, row_count):
        total = total + slots[k]
    return total, started


def gram_kernel(
    row_count, count, part, pick, out, picked, slots, total, rsend, rrecv, psend, precv, *sems
):
    row, col = lax.axis_index("row"), lax.axis_index("col")
    root = lax.rem(col, row_count)
    greet(others(row, row_count), others(col, count, 2) + [sibling_of(col)])
    value, started = row_sum(part, slots, rsend, rrecv, row_count)
    root_send(pick, row_count, root, row, picked, psend, precv.at[0])
    total[...] = value
    started += col_gather(total, out, *sems, count)
    root_wait(pick, row_count, root, row, picked, psend, precv.at[0])
    for copy in started:
        copy.wait_send()


def gram_sum(part, pick, row_count, count):
    return pl.pallas_call(
        functools.partial(gram_kernel, row_count, count),
        out_shape=[shape(count, *part.shape), shape(*pick.shape)],
        in_specs=in_vmem(2),
        out_specs=in_vmem(2),
        scratch_shapes=[
            VMEM((row_count, *part.shape), F32),
            VMEM(part.shape, F32),
            pltpu.SemaphoreType.DMA((row_count - 1,)),
            pltpu.SemaphoreType.DMA((row_count,)),
            pltpu.SemaphoreType.DMA((row_count - 1,)),
            pltpu.SemaphoreType.DMA((1,)),
            *gather_sems(count),
        ],
        compiler_params=params(1),
    )(part, pick)


def product_kernel(
    row_count, count, groups, tile_cols,
    row_terms, mirror, vectors,
    full, picked, curvature,
    terms, near, mine, far, summed, from_rows, pick, curve, slots, curve_total,
    nsend, nrecv, fsend, frecv, msend, mrecv, rsend, rrecv, psend, precv, *sems,
):
    row, col = lax.axis_index("row"), lax.axis_index("col")
    root = lax.rem(col, row_count)
    slot = col // row_count
    tile = vectors.shape[0]
    span = tile // count
    sibling = sibling_of(col)
    parity = lax.rem(col, 2)
    half = count // 2
    greet(others(row, row_count), others(col, count, 2) + [sibling])

    terms[...] = row_terms[...]

    @pl.when(row != root)
    def _():
        place = lax.rem(row - root + row_count, row_count) - 1
        copy_to("row", root, mirror, from_rows.at[place], msend, mrecv.at[place]).start()

    @pl.when(row == root)
    def _():
        for k in range(row_count - 1):
            copy_to(
                "row", lax.rem(root + k + 1, row_count), mirror, from_rows.at[k], msend, mrecv.at[k]
            ).wait_recv()
        for k in range(tile_cols):
            at = k * groups + slot
            cols = pl.ds(k * tile, tile)
            value = mirror[:, cols]
            for other in range(row_count - 1):
                value = value + from_rows[other, :, cols]
            where = pl.ds(pl.multiple_of(at * tile, tile), tile)
            terms[:, where] += value

    started = []
    for k in range(half):
        j = 2 * k + 1 - parity
        copy = copy_to(
            "col", sibling, terms.at[pl.ds(pl.multiple_of(j * span, span), span)], near.at[k],
            nsend.at[k], nrecv.at[k],
        )
        copy.start()
        started.append(copy)
    for k in range(half):
        copy_to("col", sibling, near.at[k], near.at[k], nsend.at[k], nrecv.at[k]).wait_recv()
        j = 2 * k + parity
        mine[k] = terms[pl.ds(pl.multiple_of(j * span, span), span), :] + near[k]
    place = col // 2
    for k in range(1, half):
        peer = lax.rem(place + k, half)
        copy = copy_to(
            "col", 2 * peer + parity, mine.at[peer], far.at[place], fsend.at[k - 1], frecv.at[place]
        )
        copy.start()
        started.append(copy)
    total = mine[place]
    for k in range(1, half):
        peer = lax.rem(place + k, half)
        copy_to("col", sibling, mine.at[0], far.at[peer], fsend.at[0], frecv.at[peer]).wait_recv()
        total = total + far[peer]
    summed[...] = total

    curve[...] = dot(vectors[...], total, NT)
    started += col_gather(summed, full, *sems[:4], count)
    for k in range(tile_cols):
        at = k * groups + slot
        where = pl.ds(pl.multiple_of(at * tile, tile), tile)
        for j in range(count):
            pick[pl.ds(j * span, span), pl.ds(k * tile, tile)] = full[j, :, where]
    value, more = row_sum(curve, slots, rsend, rrecv, row_count)
    started += more
    root_send(pick, row_count, root, row, picked, psend, precv.at[0])
    curve_total[...] = value
    started += col_gather(curve_total, curvature, *sems[4:], count)
    root_wait(pick, row_count, root, row, picked, psend, precv.at[0])
    for copy in started:
        copy.wait_send()

    @pl.when(row != root)
    def _():
        copy_to("row", root, mirror, from_rows.at[0], msend, mrecv.at[0]).wait_send()


def product_sums(terms, mirror, vectors, row_count, count, groups, tile_cols):
    tile = terms.shape[0]
    span = tile // count
    half = count // 2
    width = terms.shape[1]
    dma = pltpu.SemaphoreType.DMA
    return pl.pallas_call(
        functools.partial(product_kernel, row_count, count, groups, tile_cols),
        out_shape=[shape(count, span, width), shape(*mirror.shape), shape(count, tile, span)],
        in_specs=in_vmem(3),
        out_specs=in_vmem(3),
        scratch_shapes=[
            VMEM(terms.shape, F32),
            VMEM((half, span, width), F32),
            VMEM((half, span, width), F32),
            VMEM((half, span, width), F32),
            VMEM((span, width), F32),
            VMEM((row_count - 1, *mirror.shape), F32),
            VMEM(mirror.shape, F32),
            VMEM((tile, span), F32),
            VMEM((row_count, tile, span), F32),
            VMEM((tile, span), F32),
            dma((half,)),
            dma((half,)),
            dma((half,)),
            dma((half,)),
            dma,
            dma((row_count - 1,)),
            dma((row_count - 1,)),
            dma((row_count,)),
            dma((row_count - 1,)),
            dma((1,)),
            *gather_sems(count),
            *gather_sems(count),
        ],
        compiler_params=params(2),
    )(terms, mirror, vectors)


def pick_slots(block_t, tile_cols, groups, slot_index):
    leading = block_t.shape[0]
    shaped = block_t.reshape(leading, tile_cols, groups, block_t.shape[1] // (tile_cols * groups))
    picked = lax.dynamic_index_in_dim(shaped, slot_index, 2, keepdims=False)
    return picked.reshape(leading, -1)


def body(matrix, panel_t):
    tile_rows = matrix.shape[0]
    tile = matrix.shape[2]
    tile_cols = matrix.shape[3]
    row_count = lax.axis_size("row")
    col_count = lax.axis_size("col")
    row_index = lax.axis_index("row")
    col_index = lax.axis_index("col")
    groups = col_count // row_count
    slot_index = col_index // row_count
    local_rows = tile_rows * tile
    local_cols = tile_cols * tile
    span = tile // col_count
    stored = matrix.reshape(local_rows, local_cols)
    identity = jnp.eye(tile, dtype=F32)
    mine = panel_t.reshape(span, local_rows)

    panel_r = gather_panel(mine, col_count).reshape(tile, local_rows)
    part = dot(mine, panel_r, NT)
    top = jnp.where(row_index == 0, mine[:, :tile], 0.0)
    sums, panel_c = gram_sum(
        jnp.concatenate([part, top], axis=1),
        pick_slots(panel_r, tile_cols, groups, slot_index),
        row_count,
        col_count,
    )
    sums = sums.reshape(tile, 2 * tile)
    band_block, inverse, reflector = panel_factors(sums[:, :tile], sums[:, tile:])

    def with_identity(value, flag):
        head = value[:, :tile] + jnp.where(flag, identity, 0.0)
        return jnp.concatenate([head, value[:, tile:]], axis=1)

    vectors_r = with_identity(dot(inverse, panel_r, NN, HIGH), row_index == 0)
    vectors_c = with_identity(dot(inverse, panel_c, NN, HIGH), col_index == 0)

    row_numbers = jnp.arange(local_rows)
    col_numbers = jnp.arange(local_cols)
    global_row = (row_numbers // tile * row_count + row_index) * tile + row_numbers % tile
    global_col = (col_numbers // tile * col_count + col_index) * tile + col_numbers % tile
    on_lower = global_row[:, None] >= global_col[None, :]
    lower_part = jnp.where(on_lower, stored, 0.0)
    strict_part = jnp.where(global_row[:, None] > global_col[None, :], stored, 0.0)
    terms = dot(vectors_c, lower_part, NT, HIGH)
    mirror = dot(vectors_r, strict_part, NN, HIGH)
    full, products_c, curvature = product_sums(
        terms, mirror, vectors_r, row_count, col_count, groups, tile_cols
    )
    products_r = full.reshape(tile, local_rows)
    curvature = curvature.transpose(1, 0, 2).reshape(tile, tile)
    mixed = dot(dot(reflector, curvature, TN), reflector, NN)
    update_r = dot(reflector, products_r, TN, HIGH) - 0.5 * dot(mixed, vectors_r, TN, HIGH)
    update_c = dot(reflector, products_c, TN, HIGH) - 0.5 * dot(mixed, vectors_c, TN, HIGH)
    correction = dot(
        jnp.concatenate([vectors_r, update_r], axis=0),
        jnp.concatenate([update_c, vectors_c], axis=0),
        TN,
        HIGH,
    )
    updated = jnp.where(on_lower, stored - correction, 0.0).reshape(matrix.shape)
    vectors_out = lax.dynamic_slice_in_dim(vectors_r, col_index * span, span, 0).reshape(
        panel_t.shape
    )
    return (updated, vectors_out, band_block, reflector)


def solution(mesh):
    placed = (P(None, "row", None, None, "col", None), P("col", None, "row", None))
    return jax.shard_map(
        body,
        mesh=mesh,
        in_specs=placed,
        out_specs=(P(None, "row", None, None, "col", None), P("col", None, "row", None), P(), P()),
        check_vma=False,
    )
```

time: 466 us -> 193 us (0.41)
  the two profiles are of different devices: /device:TPU:0 before, /device:TPU:29 now
where the time goes in v1:
time: 193 us; the launch traced here: 189 us
  Pallas kernels  153 us (79%)
  matrix products  13.2 us (7%)
  local copies, waits for them, and re-layouts  11.4 us (6%)
  other arithmetic  10.5 us (5%)
    pallas_call x1, Pallas kernels, product_sums(): pl.pallas_call(functools.partial(product_kernel, row_count, count, groups...  79.7 us
    pallas_call x1, Pallas kernels, gram_sum(): pl.pallas_call(functools.partial(gram_kernel, row_count, count), out_shap...  32.9 us
    pallas_call x1, Pallas kernels, panel_factors(): pl.pallas_call(panel_kernel, out_shape=[shape(size, size)] * 3, in_specs=...  29.2 us
    dot_general x12, matrix products, dot(): lax.dot_general(a, b, (over, ((), ())), precision=precision, preferred_el...  13.2 us
    pallas_call x1, Pallas kernels, gather_panel(): pl.pallas_call(functools.partial(gather_kernel, count), out_shape=shape(c...  11 us
    unnamed x2, other arithmetic  10.3 us
    reshape x1, local copies, waits for them, and re-layouts, body(): jnp.where(on_lower, stored - correction, 0.0).reshape(matrix.shape)  4.7 us

profile of v1, /device:TPU:29, one launch (start us, length us, event | category | flops | bytes accessed | tf_op | source)
XLA Modules:
  0.0 189.4 jit_solution(6314414030492935940)
XLA Ops:
  0.7 1.2 reduce.1
  1.9 11.0 %shard_map.57 = f32[8,32,1024]{2,1,0:T(8,128)S(1)} custom-call(f32[32,1024]{1,0:T(8,128)S(1)} %bitcast.31), custom_call_target="tpu_custom_call" | custom-call | tf_op jit(solution)/shard_map/pallas_call | solution.py:191
  12.9 0.9 reshape_reshape.3
  13.8 1.8 dynamic-slice_reduce_fusion
  15.6 1.0 fusion.56
  16.7 32.9 %shard_map.58 = (f32[8,32,512]{2,1,0:T(8,128)S(1)}, f32[256,512]{1,0:T(8,128)S(1)}) custom-call(f32[32,512]{1,0:T(8,128)S(1)} %pad_maximum_fusion.4.part, f32[256,512]{1,0:T(8,128)S(1)} %bitcast.30), custom_call_target="tpu_custom_call" | custom-call | tf_op jit(solution)/shard_map/pallas_call | solution.py:256
  49.6 29.2 %shard_map.59 = (f32[256,256]{1,0:T(8,128)}, f32[256,256]{1,0:T(8,128)S(1)}, f32[256,256]{1,0:T(8,128)}) custom-call(f32[256,256]{1,0:T(8,128)S(1)} %get-tuple-element.31.gram_ref, f32[256,256]{1,0:T(8,128)S(1)} %get-tuple-element.30.top_ref), custom_call_target="tpu_custom_call" | custom-call | tf_op jit(solution)/shard_map/pallas_call | solution.py:105
  78.8 0.6 fusion.57
  79.4 0.4 fusion.58
  79.8 0.1 fusion.26
  79.9 0.0 copy-start.6
  79.9 0.0 copy-start.8
  79.9 0.1 slice.32
  80.0 0.0 copy-start.2
  80.0 0.1 pad_maximum_fusion.vectors
  80.2 9.0 %reduce = f32[4,256,2,256]{3,2,1,0:T(2,128)} reduce(f32[4,1,256,2,1,256]{5,4,3,2,1,0:T(1,128)} %param.2, f32[]{:T(128)} %constant.91), dimensions={1,4}, to_apply=%param.2.reduce_sub_computation | reduce | bytes 4194308 | tf_op args[0]
  89.2 1.8 copy.12
  90.9 0.0 copy-start
  91.0 0.0 copy-done.2
  91.0 1.2 fusion.7.mirror
  92.2 0.0 copy-done.6
  92.2 0.0 copy-done.8
  92.2 0.1 copy-done
  92.3 1.2 fusion.row_terms
  93.5 0.0 copy-start.4
  93.5 79.7 %shard_map.60 = (f32[8,32,1024]{2,1,0:T(8,128)S(1)}, f32[256,512]{1,0:T(8,128)S(1)}, f32[8,256,32]{2,1,0:T(8,128)S(1)}) custom-call(f32[256,1024]{1,0:T(8,128)S(1)} %fusion.row_terms, f32[256,512]{1,0:T(8,128)S(1)} %fusion.7.mirror, f32[256,1024]{1,0:T(8,128)S(1)} %pad_maximum_fusion.vectors), custom_call_target="tpu_custom_call" | custom-call | tf_op jit(solution)/shard_map/pallas_call | solution.py:368
  173.2 0.0 copy-start.5
  173.2 0.0 copy-done.4
  173.2 1.2 fusion.62
  174.5 0.3 copy.9
  174.8 0.0 copy-done.5
  174.8 0.6 fusion.60
  175.4 0.4 fusion.61
  175.8 0.0 copy-start.3
  175.8 1.7 fusion.13
  177.5 0.6 fusion.59
  178.1 0.0 copy-done.3
  178.1 0.0 copy-start.1
  178.2 0.0 copy-start.7
  178.2 0.0 copy-start.9
  178.2 0.7 fusion.12
  178.8 0.9 copy-done.1
  179.7 0.0 copy-done.7
  179.7 0.1 copy-done.9
  179.8 3.6 %compare_select_fusion = f32[1024,512]{1,0:T(8,128)} fusion(f32[1024,512]{1,0:T(8,128)S(1)} %bitcast.39, f32[256,1024]{1,0:T(8,128)S(1)} %fusion.12, f32[256,768]{1,0:T(8,128)S(1)} %copy-done.3, f32[256,256]{1,0:T(8,128)S(1)} %get-tuple-element.32, f32[256,256]{1,0:T(8,128)S(1)} %copy-done.9, f32[256,256]{1,0:T(8,128)S(1)} %copy-done.7, ...), kind=kOutput, calls=%fused_computation | convolution fusion | flops 1613758464 | bytes 7346176 | tf_op jit(solution)/shard_map/dot_general | solution.py:19
  183.4 4.7 %reshape.93 = f32[4,1,256,2,1,256]{5,4,3,2,1,0:T(1,128)} reshape(f32[1024,512]{1,0:T(8,128)} %compare_select_fusion) | data formatting | bytes 4194304 | tf_op jit(solution)/shard_map/reshape | solution.py:467
  188.1 0.8 reshape.92
  (8 shorter events, 0.1 us)
Async XLA Ops:
  79.9 12.3 %copy-start.6 = (f32[256,256]{1,0:T(8,128)}, f32[256,256]{1,0:T(8,128)S(1)}, u32[]{:S(2)}) copy-start(f32[256,256]{1,0:T(8,128)S(1)} %get-tuple-element.28) | copy-start | bytes 786436
  79.9 12.3 %copy-start.8 = (f32[256,256]{1,0:T(8,128)}, f32[256,256]{1,0:T(8,128)S(1)}, u32[]{:S(2)}) copy-start(f32[256,256]{1,0:T(8,128)S(1)} %get-tuple-element.29) | copy-start | bytes 786436
  80.0 11.0 %copy-start.2 = (f32[256,768]{1,0:T(8,128)}, f32[256,768]{1,0:T(8,128)S(1)}, u32[]{:S(2)}) copy-start(f32[256,768]{1,0:T(8,128)S(1)} %slice.32) | copy-start | bytes 2359300
  90.9 1.3 copy-start
  93.5 79.8 %copy-start.4 = (f32[256,256]{1,0:T(8,128)S(1)}, f32[256,256]{1,0:T(8,128)}, u32[]{:S(2)}) copy-start(f32[256,256]{1,0:T(8,128)} %get-tuple-element.27) | copy-start | bytes 786436
  173.2 1.5 copy-start.5
  175.8 2.4 %copy-start.3 = (f32[256,768]{1,0:T(8,128)S(1)}, f32[256,768]{1,0:T(8,128)}, u32[]{:S(2)}) copy-start(f32[256,768]{1,0:T(8,128)} %copy-done.2) | copy-start | bytes 2359300
  178.1 1.6 copy-start.1
  178.2 1.6 copy-start.7
  178.2 1.6 copy-start.9

commit v2 on v0

v2 whole, which is shorter than its diff:
```python
import functools

import jax
import jax.numpy as jnp
from jax import lax
from jax.experimental import pallas as pl
from jax.experimental.pallas import tpu as pltpu
from jax.sharding import PartitionSpec as P

F32 = jnp.float32
VMEM = pltpu.VMEM
HIGHEST = lax.Precision.HIGHEST
BLOCK = 64
GROUP = 4


def dot(a, b, over, precision=HIGHEST):
    return lax.dot_general(a, b, (over, ((), ())), precision=precision, preferred_element_type=F32)


NN = ((1,), (0,))
TN = ((0,), (0,))
NT = ((1,), (1,))


def in_vmem(count):
    return [pl.BlockSpec(memory_space=VMEM)] * count


def params(collective=None):
    if collective is None:
        return pltpu.CompilerParams(vmem_limit_bytes=48 << 20)
    return pltpu.CompilerParams(
        vmem_limit_bytes=48 << 20, collective_id=collective, has_side_effects=True
    )


def shape(*dims):
    return jax.ShapeDtypeStruct(dims, F32)


def inverse_factor(block):
    size = block.shape[0]
    row = lax.broadcasted_iota(jnp.int32, (size, 2 * size), 0)
    col = lax.broadcasted_iota(jnp.int32, (size, 2 * size), 1)
    work = jnp.concatenate([block, jnp.zeros_like(block)], axis=1)
    work = jnp.where(col == row + size, 1.0, work)
    scale = jnp.zeros((size, 2 * size), F32)
    for first in range(0, size, GROUP):
        cols = [
            jnp.broadcast_to(work[:, first + t : first + t + 1], (size, 2 * size))
            for t in range(GROUP)
        ]
        for t in range(GROUP):
            j = first + t
            pivot = cols[t][j : j + 1, :]
            factor = jnp.where(row > j, cols[t] * (1.0 / pivot), 0.0)
            for u in range(t + 1, GROUP):
                cols[u] = cols[u] - factor * cols[u][j : j + 1, :]
            work = work - factor * work[j : j + 1, :]
            scale = jnp.where(row == j, lax.rsqrt(pivot), scale)
    return (work * scale)[:, size:]


def dot3(a, b, over):
    ah, bh = a.astype(jnp.bfloat16), b.astype(jnp.bfloat16)
    al, bl = (a - ah.astype(F32)).astype(jnp.bfloat16), (b - bh.astype(F32)).astype(jnp.bfloat16)
    one = functools.partial(dot, over=over, precision=None)
    return one(ah, bl) + one(al, bh) + one(ah, bh)


def unit(size):
    row = lax.broadcasted_iota(jnp.int32, (size, size), 0)
    return (row == lax.broadcasted_iota(jnp.int32, (size, size), 1)).astype(F32)


def factor_steps(gram, work):
    size = gram.shape[0]
    work[:, :size] = gram
    work[:, size:] = unit(size)
    for lo in range(0, size, BLOCK):
        hi = lo + BLOCK
        inv = inverse_factor(work[lo:hi, lo:hi])
        rows = dot(inv, work[lo:hi, :], NN)
        work[lo:hi, :] = rows
        if hi < size:
            work[hi:, :] -= dot(rows[:, hi:size], rows, TN)
        yield


def greet(row_peers, col_peers):
    barrier = pltpu.get_barrier_semaphore()
    for peer in row_peers:
        pl.semaphore_signal(
            barrier, inc=1, device_id={"row": peer}, device_id_type=pl.DeviceIdType.MESH
        )
    for peer in col_peers:
        pl.semaphore_signal(
            barrier, inc=1, device_id={"col": peer}, device_id_type=pl.DeviceIdType.MESH
        )
    pl.semaphore_wait(barrier, len(row_peers) + len(col_peers))


def copy_to(axis, peer, src, dst, send, recv):
    return pltpu.make_async_remote_copy(
        src_ref=src,
        dst_ref=dst,
        send_sem=send,
        recv_sem=recv,
        device_id={axis: peer},
        device_id_type=pl.DeviceIdType.MESH,
    )


def others(me, count, step=1):
    return [lax.rem(me + k, count) for k in range(step, count, step)]


def sibling_of(me):
    return me + 1 - 2 * lax.rem(me, 2)


class Gather:
    def __init__(self, src, out, sems, count):
        self.src, self.out, self.count = src, out, count
        self.near_send, self.near_recv, self.far_send, self.far_recv = sems
        self.me = lax.axis_index("col")
        self.sibling = sibling_of(self.me)
        self.started = []

    def near(self, src, slot):
        return copy_to(
            "col", self.sibling, src, self.out.at[slot], self.near_send.at[slot],
            self.near_recv.at[slot],
        )

    def far(self, peer, slot, k):
        return copy_to(
            "col", peer, self.src, self.out.at[slot], self.far_send.at[k], self.far_recv.at[slot]
        )

    def start(self):
        for k, peer in enumerate(others(self.me, self.count, 2)):
            self.started.append(self.far(peer, self.me, k))
            self.started[-1].start()
        self.started.append(self.near(self.src, self.me))
        self.started[-1].start()
        self.out[self.me] = self.src[...]

    def finish(self):
        for peer in others(self.me, self.count, 2):
            self.far(peer, peer, 0).wait_recv()
            self.started.append(self.near(self.out.at[peer], peer))
            self.started[-1].start()
        for k in range(0, self.count, 2):
            self.near(self.src, lax.rem(self.sibling + k, self.count)).wait_recv()

    def drain(self):
        for copy in self.started:
            copy.wait_send()


class RowSum:
    def __init__(self, src, slots, send, recv, count):
        self.src, self.slots, self.send, self.recv, self.count = src, slots, send, recv, count
        self.me = lax.axis_index("row")

    def copy(self, peer, slot, k):
        return copy_to(
            "row", peer, self.src, self.slots.at[slot], self.send.at[k], self.recv.at[slot]
        )

    def start(self):
        for k, peer in enumerate(others(self.me, self.count)):
            self.copy(peer, self.me, k).start()
        self.slots[self.me] = self.src[...]

    def finish(self):
        for peer in others(self.me, self.count):
            self.copy(peer, peer, 0).wait_recv()

    def total(self):
        total = self.slots[0]
        for k in range(1, self.count):
            total = total + self.slots[k]
        return total

    def drain(self):
        for k, peer in enumerate(others(self.me, self.count)):
            self.copy(peer, self.me, k).wait_send()


DMA = pltpu.SemaphoreType.DMA


def gather_sems(count):
    return [DMA((count,)), DMA((count,)), DMA((count // 2,)), DMA((count,))]


def row_sems(count):
    return [DMA((count - 1,)), DMA((count,))]


def panel_kernel(
    row_count, count, groups, tile_cols,
    mine, panel_r, panel_c, top, band, inverse,
    panel_z, part, slots, part_total, gram, work, csend, crecv, *sems,
):
    row, col = lax.axis_index("row"), lax.axis_index("col")
    span = mine.shape[0]
    tile = span * count
    peers = others(col, count)
    greet(others(row, row_count), peers)
    gather_r = Gather(mine, panel_r, sems[0:4], count)
    gather_g = Gather(part_total, gram, sems[4:8], count)
    rows_z = RowSum(mine, panel_z, *sems[8:10], row_count)
    rows_g = RowSum(part, slots, *sems[10:12], row_count)
    gather_r.start()
    rows_z.start()
    gather_r.finish()
    part[...] = dot(mine[...], panel_r[...].reshape(tile, -1), NT)
    rows_g.start()
    rows_g.finish()
    part_total[...] = rows_g.total()
    gather_g.start()
    rows_z.finish()
    gather_g.finish()

    def tiles_for(target):
        root, slot = lax.rem(target, row_count), target // row_count
        for k in range(tile_cols):
            start = pl.multiple_of((k * groups + slot) * tile, tile)
            yield panel_z.at[root, :, pl.ds(start, tile)], pl.ds(k * tile, tile)

    started = []
    for n, peer in enumerate(peers):
        for k, (src, at) in enumerate(tiles_for(peer)):
            started.append(
                copy_to("col", peer, src, panel_c.at[col, :, at], csend.at[n, k], crecv.at[col, k])
            )
        started.append(
            copy_to(
                "col", peer, panel_z.at[0, :, pl.ds(0, tile)], top.at[col],
                csend.at[n, tile_cols], crecv.at[col, tile_cols],
            )
        )
    for copy in started:
        copy.start()
    for src, at in tiles_for(col):
        panel_c[col, :, at] = src[...]
    top[col] = panel_z[0, :, :tile]

    for _ in factor_steps(gram[...].reshape(tile, tile), work):
        pass
    keep = lax.broadcasted_iota(jnp.int32, (tile, tile), 1) >= lax.broadcasted_iota(
        jnp.int32, (tile, tile), 0
    )
    band[...] = jnp.where(keep, -work[:, :tile], 0.0)
    inverse[...] = work[:, tile:]
    for peer in peers:
        for k, (src, at) in enumerate(tiles_for(col)):
            copy_to(
                "col", peer, src, panel_c.at[peer, :, at], csend.at[0, k], crecv.at[peer, k]
            ).wait_recv()
        copy_to(
            "col", peer, top.at[col], top.at[peer], csend.at[0, 0], crecv.at[peer, tile_cols]
        ).wait_recv()
    for each in (gather_r, gather_g, rows_z, rows_g, *started):
        each.drain() if hasattr(each, "drain") else each.wait_send()


def panel_step(mine, row_count, count, groups, tile_cols):
    span, width = mine.shape
    tile = span * count
    return pl.pallas_call(
        functools.partial(panel_kernel, row_count, count, groups, tile_cols),
        out_shape=[
            shape(count, span, width),
            shape(count, span, tile_cols * tile),
            shape(count, span, tile),
            shape(tile, tile),
            shape(tile, tile),
        ],
        in_specs=in_vmem(1),
        out_specs=in_vmem(5),
        scratch_shapes=[
            VMEM((row_count, span, width), F32),
            VMEM((span, tile), F32),
            VMEM((row_count, span, tile), F32),
            VMEM((span, tile), F32),
            VMEM((count, span, tile), F32),
            VMEM((tile, 2 * tile), F32),
            DMA((count - 1, tile_cols + 1)),
            DMA((count, tile_cols + 1)),
            *gather_sems(count),
            *gather_sems(count),
            *row_sems(row_count),
            *row_sems(row_count),
        ],
        compiler_params=params(0),
    )(mine)


PARTS = 4


def product_kernel(
    row_count, count, groups, tile_cols,
    lines, panel_r, panel_c, top, inverse,
    out_r, out_c, update_r, update_c, reflector, out_mine,
    mirror, low, high, acc, near, mine, far, summed, full, picked, curve, slots, curve_total,
    curvature, work,
    chain_send, low_recv, high_recv, nsend, nrecv, fsend, frecv, up_send, down_send, precv, *sems,
):
    row, col = lax.axis_index("row"), lax.axis_index("col")
    root, slot = lax.rem(col, row_count), col // row_count
    tile, width = panel_r.shape
    halves, _, sub, _ = acc.shape
    span = tile // count
    per = tile // PARTS // sub
    sibling, parity, half = sibling_of(col), lax.rem(col, 2), count // 2
    greet(others(row, row_count), others(col, count, 2) + [sibling])

    inv = inverse[...]
    out_r[...] = dot3(inv, panel_r[...], NN)
    out_c[...] = dot3(inv, panel_c[...], NN)

    @pl.when(row == 0)
    def _():
        out_r[:, :tile] += unit(tile)

    @pl.when(col == 0)
    def _():
        out_c[:, :tile] += unit(tile)

    vectors = out_r[...]
    matrix, global_row, global_col = read_matrix(lines, width, tile, row_count, count, tile_cols)
    products = dot3(vectors, jnp.where(global_row > global_col, matrix, 0.0), NN)
    mirror[...] = products.reshape(mirror.shape)

    from_low = (row > 0) & (row <= root)
    from_high = (row < row_count - 1) & (row >= root)
    is_end = (row != root) & ((row == 0) | (row == row_count - 1))

    def hop_up(q):
        peer = jnp.minimum(row + 1, row_count - 1)
        return copy_to("row", peer, mirror.at[q], low.at[q], chain_send.at[q], low_recv.at[q])

    def hop_down(q):
        peer = jnp.maximum(row - 1, 0)
        return copy_to("row", peer, mirror.at[q], high.at[q], chain_send.at[q], high_recv.at[q])

    def hop(q, go, act):
        pl.when(go & (row < root))(lambda: act(hop_up(q)))
        pl.when(go & (row > root))(lambda: act(hop_down(q)))

    for q in range(PARTS):
        hop(q, is_end, lambda copy: copy.start())

    terms = dot3(out_c[...], jnp.where(global_row >= global_col, matrix, 0.0), NT)
    acc[...] = terms.reshape(acc.shape)
    started = []

    def chunk_of(q):
        return q * halves // PARTS, (q * per) % count

    for q in range(PARTS):

        @pl.when(from_low)
        def _():
            copy_to(
                "row", jnp.maximum(row - 1, 0), mirror.at[q], low.at[q], chain_send.at[q],
                low_recv.at[q],
            ).wait_recv()
            mirror[q] += low[q]

        @pl.when(from_high)
        def _():
            copy_to(
                "row", jnp.minimum(row + 1, row_count - 1), mirror.at[q], high.at[q],
                chain_send.at[q], high_recv.at[q],
            ).wait_recv()
            mirror[q] += high[q]

        hop(q, jnp.logical_not(is_end), lambda copy: copy.start())
        h, first = chunk_of(q)

        @pl.when(row == root)
        def _():
            for k in range(tile_cols):
                where = pl.ds(pl.multiple_of((k * groups + slot) * tile, tile), tile)
                value = mirror[q, :, k * tile : (k + 1) * tile].reshape(per, sub, tile)
                acc[h, first : first + per, :, where] += value

        if (q + 1) % (PARTS // halves) == 0:
            for k in range(half):
                j = 2 * k + 1 - parity
                started.append(
                    copy_to("col", sibling, acc.at[h, j], near.at[h, k], nsend.at[h, k], nrecv.at[h, k])
                )
                started[-1].start()

    block = dot(inv, top[...], NN) + unit(tile)
    factor = factor_steps(dot(block, block, TN), work)

    place = col // 2
    for h in range(halves):
        for k in range(half):
            copy_to(
                "col", sibling, acc.at[h, 0], near.at[h, k], nsend.at[h, k], nrecv.at[h, k]
            ).wait_recv()
            mine[h, k] = acc[h, 2 * k + parity] + near[h, k]
        for k, peer in enumerate(others(place, half)):
            started.append(
                copy_to(
                    "col", 2 * peer + parity, mine.at[h, peer], far.at[h, place], fsend.at[h, k],
                    frecv.at[h, place],
                )
            )
            started[-1].start()
    next(factor, None)

    gathers = [
        Gather(summed.at[h], full.at[h], sems[4 * h : 4 * h + 4], count) for h in range(halves)
    ]
    for h in range(halves):
        total = mine[h, place]
        for peer in others(place, half):
            copy_to(
                "col", 2 * peer + parity, mine.at[h, 0], far.at[h, peer], fsend.at[h, 0],
                frecv.at[h, peer],
            ).wait_recv()
            total = total + far[h, peer]
        summed[h] = total
        gathers[h].start()

    sems = sems[4 * halves :]
    curve[...] = dot3(summed[...].reshape(span, width), vectors, NT)
    curve_sum = RowSum(curve, slots, *sems[:2], row_count)
    curve_gather = Gather(curve_total, curvature, sems[2:6], count)
    curve_sum.start()
    next(factor, None)

    def pass_up(q):
        peer = jnp.minimum(row + 1, row_count - 1)
        return copy_to("row", peer, picked.at[q], picked.at[q], up_send.at[q], precv.at[q])

    def pass_down(q):
        peer = jnp.maximum(row - 1, 0)
        return copy_to("row", peer, picked.at[q], picked.at[q], down_send.at[q], precv.at[q])

    def pass_on(q, go, act):
        pl.when(go & (row >= root) & (row < row_count - 1))(lambda: act(pass_up(q)))
        pl.when(go & (row <= root) & (row > 0))(lambda: act(pass_down(q)))

    def pick(q):
        h, first = chunk_of(q)

        @pl.when(row == root)
        def _():
            for k in range(tile_cols):
                where = pl.ds(pl.multiple_of((k * groups + slot) * tile, tile), tile)
                value = full[h, first : first + per, :, where]
                picked[q, :, k * tile : (k + 1) * tile] = value.reshape(tile // PARTS, tile)

        pass_on(q, row == root, lambda copy: copy.start())

    for h in range(halves):
        gathers[h].finish()
        for q in range(h * PARTS // halves, (h + 1) * PARTS // halves):
            pick(q)
        if h == 0:
            curve_sum.finish()
            curve_total[...] = curve_sum.total()
            curve_gather.start()
    curve_gather.finish()
    for q in range(PARTS):
        pl.when(row > root)(lambda: pass_down(q).wait_recv())
        pl.when(row < root)(lambda: pass_up(q).wait_recv())
        pass_on(q, row != root, lambda copy: copy.start())
        if q in (0, PARTS - 1):
            next(factor, None)
    for _ in factor:
        pass

    inv2 = work[:, tile:]
    reflect = dot(inv2, dot(inv2, block, NT), TN)
    reflector[...] = reflect
    pieces = curvature[...]
    curvature_t = jnp.concatenate(
        [pieces[:, h * sub : (h + 1) * sub].reshape(tile // halves, tile) for h in range(halves)],
        axis=0,
    )
    mixed = -0.5 * dot(dot(reflect, curvature_t, TN), reflect, NN)
    update_r[...] = dot3(reflect, full[...].reshape(tile, width), TN) + dot3(mixed, vectors, NN)
    update_c[...] = dot3(reflect, picked[...].reshape(tile, -1), TN) + dot3(mixed, out_c[...], NN)
    out_mine[...] = out_r[pl.ds(pl.multiple_of(col * span, span), span), :]

    for q in range(PARTS):
        hop(q, row != root, lambda copy: copy.wait_send())
        pass_on(q, row >= 0, lambda copy: copy.wait_send())
    curve_sum.drain()
    for each in (*gathers, curve_gather):
        each.drain()
    for copy in started:
        copy.wait_send()


def read_matrix(lines, rows, tile, row_count, count, tile_cols):
    row, col = lax.axis_index("row"), lax.axis_index("col")
    strips = tile_cols * tile // 128
    matrix = jnp.concatenate(
        [lines[pl.ds(k, rows, stride=strips), :] for k in range(strips)], axis=1
    )
    r = lax.broadcasted_iota(jnp.int32, matrix.shape, 0)
    c = lax.broadcasted_iota(jnp.int32, matrix.shape, 1)
    global_row = (r // tile * row_count + row) * tile + r % tile
    global_col = (c // tile * count + col) * tile + c % tile
    return matrix, global_row, global_col


def product_step(lines, panel_r, panel_c, top, inverse, row_count, count, groups, tile_cols):
    tile, width = panel_r.shape
    cols = panel_c.shape[1]
    span, half = tile // count, count // 2
    halves = 2 if span % 16 == 0 else 1
    sub = span // halves
    part = (PARTS, tile // PARTS, cols)
    return pl.pallas_call(
        functools.partial(product_kernel, row_count, count, groups, tile_cols),
        out_shape=[
            shape(tile, width),
            shape(tile, cols),
            shape(tile, width),
            shape(tile, cols),
            shape(tile, tile),
            shape(span, width),
        ],
        in_specs=in_vmem(5),
        out_specs=in_vmem(6),
        scratch_shapes=[
            VMEM(part, F32),
            VMEM(part, F32),
            VMEM(part, F32),
            VMEM((halves, count, sub, width), F32),
            VMEM((halves, half, sub, width), F32),
            VMEM((halves, half, sub, width), F32),
            VMEM((halves, half, sub, width), F32),
            VMEM((halves, sub, width), F32),
            VMEM((halves, count, sub, width), F32),
            VMEM(part, F32),
            VMEM((span, tile), F32),
            VMEM((row_count, span, tile), F32),
            VMEM((span, tile), F32),
            VMEM((count, span, tile), F32),
            VMEM((tile, 2 * tile), F32),
            DMA((PARTS,)),
            DMA((PARTS,)),
            DMA((PARTS,)),
            DMA((halves, half)),
            DMA((halves, half)),
            DMA((halves, half)),
            DMA((halves, half)),
            DMA((PARTS,)),
            DMA((PARTS,)),
            DMA((PARTS,)),
            *(gather_sems(count) * halves),
            *row_sems(row_count),
            *gather_sems(count),
        ],
        compiler_params=params(1),
    )(lines, panel_r, panel_c, top, inverse)


def update_kernel(row_count, count, tile_cols, where, lines, yr, xr, yc, xc, out):
    tile = yr.shape[0]
    strips = tile_cols * tile // 128
    step = pl.program_id(0)
    left = jnp.concatenate([yr[...], xr[...]], axis=0)
    right = jnp.concatenate([xc[...], yc[...]], axis=0)
    correction = dot3(left, right, TN)
    r = lax.broadcasted_iota(jnp.int32, (tile, 128), 0)
    c = lax.broadcasted_iota(jnp.int32, (tile, 128), 1)
    global_row = (step * row_count + where[0]) * tile + r
    for k in range(strips):
        first = (k * 128 // tile * count + where[1]) * tile + k * 128 % tile
        rows = pl.ds(k, tile, stride=strips)
        value = lines[rows, :] - correction[:, k * 128 : (k + 1) * 128]
        out[rows, :] = jnp.where(global_row >= first + c, value, 0.0)


def update_step(where, lines, yr, xr, yc, xc, row_count, count, tile_cols):
    tile, width = yr.shape
    steps = width // tile
    block = (lines.shape[0] // steps, 128)
    strip = pl.BlockSpec((tile, tile), lambda i: (0, i))
    whole = pl.BlockSpec(yc.shape, lambda i: (0, 0))
    lined = pl.BlockSpec(block, lambda i: (i, 0))
    return pl.pallas_call(
        functools.partial(update_kernel, row_count, count, tile_cols),
        grid=(steps,),
        out_shape=shape(*lines.shape),
        in_specs=[pl.BlockSpec(memory_space=pltpu.SMEM), lined, strip, strip, whole, whole],
        out_specs=lined,
        compiler_params=params(),
    )(where, lines, yr, xr, yc, xc)


def body(matrix, panel_t):
    tile_rows, _, tile, tile_cols = matrix.shape[:4]
    row_count, count = lax.axis_size("row"), lax.axis_size("col")
    groups = count // row_count
    span, width = tile // count, tile_rows * tile
    lines = matrix.reshape(-1, 128)
    sizes = (row_count, count, groups, tile_cols)
    panel_r, panel_c, top, band_block, inverse = panel_step(panel_t.reshape(span, width), *sizes)
    yr, yc, xr, xc, reflector, vectors = product_step(
        lines,
        panel_r.reshape(tile, width),
        panel_c.reshape(tile, -1),
        top.reshape(tile, tile),
        inverse,
        *sizes,
    )
    where = jnp.stack([lax.axis_index("row"), lax.axis_index("col")])
    updated = update_step(where, lines, yr, xr, yc, xc, row_count, count, tile_cols)
    return (updated.reshape(matrix.shape), vectors.reshape(panel_t.shape), band_block, reflector)


def solution(mesh):
    placed = (P(None, "row", None, None, "col", None), P("col", None, "row", None))
    return jax.shard_map(
        body,
        mesh=mesh,
        in_specs=placed,
        out_specs=(P(None, "row", None, None, "col", None), P("col", None, "row", None), P(), P()),
        check_vma=False,
    )
```

time: 466 us -> 113 us (0.24)
  the two profiles are of different devices: /device:TPU:0 before, /device:TPU:3 now
where the time goes in v2:
time: 113 us
  Pallas kernels  109 us (96%)
  local copies, waits for them, and re-layouts  2.24 us (2%)
  other arithmetic  1.32 us (1%)
    pallas_call x1, Pallas kernels, product_step(): pl.pallas_call(functools.partial(product_kernel, row_count, count, groups...  66.5 us
    pallas_call x1, Pallas kernels, panel_step(): pl.pallas_call(functools.partial(panel_kernel, row_count, count, groups,...  38 us
    pallas_call x1, Pallas kernels, update_step(): pl.pallas_call(functools.partial(update_kernel, row_count, count, tile_co...  4.1 us

profile of v2, /device:TPU:3, one launch (start us, length us, event | category | flops | bytes accessed | tf_op | source)
XLA Modules:
  0.0 112.9 jit_solution(9393065164886047923)
XLA Ops:
  0.6 0.1 pad_add_fusion.where
  0.7 1.2 %reduce = f32[32,4,256]{2,1,0:T(4,128)S(1)} reduce(f32[32,4,1,256]{3,2,1,0:T(1,128)} %param.3, f32[]{:T(128)} %constant.10), dimensions={2}, to_apply=%param.3.reduce_sub_computation | reduce | bytes 262148 | tf_op args[1]
  2.0 38.0 %shard_map.57 = (f32[8,32,1024]{2,1,0:T(8,128)S(1)}, f32[8,32,512]{2,1,0:T(8,128)S(1)}, f32[8,32,256]{2,1,0:T(8,128)S(1)}, f32[256,256]{1,0:T(8,128)S(1)}, f32[256,256]{1,0:T(8,128)S(1)}) custom-call(f32[32,1024]{1,0:T(8,128)S(1)} %bitcast.12), custom_call_target="tpu_custom_call" | custom-call | tf_op jit(solution)/shard_map/pallas_call | solution.py:275
  40.0 0.0 copy-start
  40.0 66.5 %shard_map.58 = (f32[256,1024]{1,0:T(8,128)S(1)}, f32[256,512]{1,0:T(8,128)S(1)}, f32[256,1024]{1,0:T(8,128)S(1)}, f32[256,512]{1,0:T(8,128)S(1)}, f32[256,256]{1,0:T(8,128)S(1)}, /*index=5*/f32[32,1024]{1,0:T(8,128)S(1)}) custom-call(f32[4096,128]{1,0:T(8,128)} %bitcast.9, f32[256,1024]{1,0:T(8,128)S(1)} %bitcast.11, f32[256,512]{1,0:T(8,128)S(1)} %bitcast.13, ...), custom_call_target="tpu_custom_call" | custom-call | tf_op jit(solution)/shard_map/pallas_call | solution.py:529
  106.5 0.0 copy-done
  106.6 4.1 %shard_map.59 = f32[4096,128]{1,0:T(8,128)} custom-call(s32[2]{0:T(128)S(1)} %pad_add_fusion.where, f32[4096,128]{1,0:T(8,128)S(1)} %bitcast.10, f32[256,1024]{1,0:T(8,128)S(1)} %get-tuple-element.19.yr, f32[256,1024]{1,0:T(8,128)S(1)} %get-tuple-element.20.xr, f32[256,512]{1,0:T(8,128)S(1)} %get-tuple-element.21.yc, f32[256,512]{1,0:T(8,128)S(1)} %get-tuple-element.22.xc), custom_call_target="tpu_custom_call" | custom-call | tf_op jit(solution)/shard_map/pallas_call | solution.py:599
  110.7 0.8 reshape.36
  111.5 0.7 copy.11
  112.2 0.7 copy.12
  (1 shorter events, 0.0 us)
Async XLA Ops:
  40.0 66.5 %copy-start = (f32[4,1,256,2,1,256]{5,4,3,2,1,0:T(1,128)S(1)}, f32[4,1,256,2,1,256]{5,4,3,2,1,0:T(1,128)}, u32[]{:S(2)}) copy-start(f32[4,1,256,2,1,256]{5,4,3,2,1,0:T(1,128)} %param.2) | copy-start | bytes 6291460

commit v3 on v2

--- a/solution.py
+++ b/solution.py
@@ -54,7 +54,8 @@
         for t in range(GROUP):
             j = first + t
             pivot = cols[t][j : j + 1, :]
-            factor = jnp.where(row > j, cols[t] * (1.0 / pivot), 0.0)
+            guess = pl.reciprocal(pivot, approx=True)
+            factor = jnp.where(row > j, cols[t] * (guess * (2.0 - pivot * guess)), 0.0)
             for u in range(t + 1, GROUP):
                 cols[u] = cols[u] - factor * cols[u][j : j + 1, :]
             work = work - factor * work[j : j + 1, :]
@@ -203,13 +204,20 @@
 
 def panel_kernel(
     row_count, count, groups, tile_cols,
-    mine, panel_r, panel_c, top, band, inverse,
-    panel_z, part, slots, part_total, gram, work, csend, crecv, *sems,
+    own_lines, lines_hbm, panel_r, panel_c, top, band, inverse, mirror_sum,
+    mine, lines, mirror, from_rows, panel_z, part, slots, part_total, gram, work,
+    load, msend, mrecv, csend, crecv, *sems,
 ):
     row, col = lax.axis_index("row"), lax.axis_index("col")
-    span = mine.shape[0]
+    span, width = mine.shape
     tile = span * count
     peers = others(col, count)
+    root = lax.rem(col, row_count)
+    fetch = pltpu.make_async_copy(lines_hbm, lines, load)
+    fetch.start()
+    strips = width // 128
+    for k in range(strips):
+        mine[:, k * 128 : (k + 1) * 128] = own_lines[pl.ds(k, span, stride=strips), :]
     greet(others(row, row_count), peers)
     gather_r = Gather(mine, panel_r, sems[0:4], count)
     gather_g = Gather(part_total, gram, sems[4:8], count)
@@ -220,11 +228,22 @@
     gather_r.finish()
     part[...] = dot(mine[...], panel_r[...].reshape(tile, -1), NT)
     rows_g.start()
+    fetch.wait()
+    matrix, global_row, global_col = read_matrix(lines, width, tile, row_count, count, tile_cols)
+    strict = jnp.where(global_row > global_col, matrix, 0.0)
+    mirror[...] = dot3(panel_r[...].reshape(tile, width), strict, NN)
     rows_g.finish()
     part_total[...] = rows_g.total()
     gather_g.start()
     rows_z.finish()
     gather_g.finish()
+
+    place = jnp.maximum(lax.rem(row - root + row_count, row_count) - 1, 0)
+
+    def to_root():
+        return copy_to("row", root, mirror, from_rows.at[place], msend, mrecv.at[place])
+
+    pl.when(row != root)(lambda: to_root().start())
 
     def tiles_for(target):
         root, slot = lax.rem(target, row_count), target // row_count
@@ -255,8 +274,10 @@
     keep = lax.broadcasted_iota(jnp.int32, (tile, tile), 1) >= lax.broadcasted_iota(
         jnp.int32, (tile, tile), 0
     )
-    band[...] = jnp.where(keep, -work[:, :tile], 0.0)
+    upper = jnp.where(keep, work[:, :tile], 0.0)
+    band[...] = -upper
     inverse[...] = work[:, tile:]
+    factor = upper.T
     for peer in peers:
         for k, (src, at) in enumerate(tiles_for(col)):
             copy_to(
@@ -268,10 +289,38 @@
     for each in (gather_r, gather_g, rows_z, rows_g, *started):
         each.drain() if hasattr(each, "drain") else each.wait_send()
 
-
-def panel_step(mine, row_count, count, groups, tile_cols):
-    span, width = mine.shape
-    tile = span * count
+    @pl.when(row == 0)
+    def _():
+        panel_r[:, :, :tile] += factor.reshape(count, span, tile)
+
+    @pl.when(col == 0)
+    def _():
+        panel_c[:, :, :tile] += factor.reshape(count, span, tile)
+
+    @pl.when(row != root)
+    def _():
+        to_root().wait_send()
+        mirror_sum[...] = mirror[...]
+
+    @pl.when(row == root)
+    def _():
+        total = mirror[...]
+        for k in range(row_count - 1):
+            copy_to(
+                "row", lax.rem(root + k + 1, row_count), mirror, from_rows.at[k], msend, mrecv.at[k]
+            ).wait_recv()
+            total = total + from_rows[k]
+        mirror_sum[...] = total
+
+    @pl.when((row == 0) & (col == 0))
+    def _():
+        mirror_sum[:, :tile] += dot3(factor, strict[:tile, :tile], NN)
+
+
+def panel_step(own_lines, lines, tile, row_count, count, groups, tile_cols):
+    span = tile // count
+    width = own_lines.shape[0] * 128 // span
+    cols = tile_cols * tile
     return pl.pallas_call(
         functools.partial(panel_kernel, row_count, count, groups, tile_cols),
         out_shape=[
@@ -280,16 +329,24 @@
             shape(count, span, tile),
             shape(tile, tile),
             shape(tile, tile),
+            shape(tile, cols),
         ],
-        in_specs=in_vmem(1),
-        out_specs=in_vmem(5),
+        in_specs=in_vmem(1) + [pl.BlockSpec(memory_space=pl.ANY)],
+        out_specs=in_vmem(6),
         scratch_shapes=[
+            VMEM((span, width), F32),
+            VMEM(lines.shape, F32),
+            VMEM((tile, cols), F32),
+            VMEM((row_count - 1, tile, cols), F32),
             VMEM((row_count, span, width), F32),
             VMEM((span, tile), F32),
             VMEM((row_count, span, tile), F32),
             VMEM((span, tile), F32),
             VMEM((count, span, tile), F32),
             VMEM((tile, 2 * tile), F32),
+            DMA,
+            DMA,
+            DMA((row_count - 1,)),
             DMA((count - 1, tile_cols + 1)),
             DMA((count, tile_cols + 1)),
             *gather_sems(count),
@@ -298,7 +355,7 @@
             *row_sems(row_count),
         ],
         compiler_params=params(0),
-    )(mine)
+    )(own_lines, lines)
 
 
 PARTS = 4
@@ -306,11 +363,10 @@
 
 def product_kernel(
     row_count, count, groups, tile_cols,
-    lines, panel_r, panel_c, top, inverse,
+    lines, panel_r, panel_c, top, inverse, mirror,
     out_r, out_c, update_r, update_c, reflector, out_mine,
-    mirror, low, high, acc, near, mine, far, summed, full, picked, curve, slots, curve_total,
-    curvature, work,
-    chain_send, low_recv, high_recv, nsend, nrecv, fsend, frecv, up_send, down_send, precv, *sems,
+    acc, near, mine, far, summed, full, picked, curve, slots, curve_total, curvature, work,
+    nsend, nrecv, fsend, frecv, up_send, down_send, precv, *sems,
 ):
     row, col = lax.axis_index("row"), lax.axis_index("col")
     root, slot = lax.rem(col, row_count), col // row_count
@@ -321,85 +377,32 @@
     sibling, parity, half = sibling_of(col), lax.rem(col, 2), count // 2
     greet(others(row, row_count), others(col, count, 2) + [sibling])
 
+    matrix, global_row, global_col = read_matrix(lines, width, tile, row_count, count, tile_cols)
+    lower = jnp.where(global_row >= global_col, matrix, 0.0)
+    acc[...] = dot3(panel_c[...], lower, NT).reshape(acc.shape)
+    started = []
+
+    def chunk_of(q):
+        return q * halves // PARTS, (q * per) % count
+
+    @pl.when(row == root)
+    def _():
+        for k in range(tile_cols):
+            where = pl.ds(pl.multiple_of((k * groups + slot) * tile, tile), tile)
+            value = mirror[:, k * tile : (k + 1) * tile].reshape(halves, count, sub, tile)
+            acc[:, :, :, where] += value
+
+    for h in range(halves):
+        for k in range(half):
+            j = 2 * k + 1 - parity
+            started.append(
+                copy_to("col", sibling, acc.at[h, j], near.at[h, k], nsend.at[h, k], nrecv.at[h, k])
+            )
+            started[-1].start()
+
     inv = inverse[...]
     out_r[...] = dot3(inv, panel_r[...], NN)
-    out_c[...] = dot3(inv, panel_c[...], NN)
-
-    @pl.when(row == 0)
-    def _():
-        out_r[:, :tile] += unit(tile)
-
-    @pl.when(col == 0)
-    def _():
-        out_c[:, :tile] += unit(tile)
-
     vectors = out_r[...]
-    matrix, global_row, global_col = read_matrix(lines, width, tile, row_count, count, tile_cols)
-    products = dot3(vectors, jnp.where(global_row > global_col, matrix, 0.0), NN)
-    mirror[...] = products.reshape(mirror.shape)
-
-    from_low = (row > 0) & (row <= root)
-    from_high = (row < row_count - 1) & (row >= root)
-    is_end = (row != root) & ((row == 0) | (row == row_count - 1))
-
-    def hop_up(q):
-        peer = jnp.minimum(row + 1, row_count - 1)
-        return copy_to("row", peer, mirror.at[q], low.at[q], chain_send.at[q], low_recv.at[q])
-
-    def hop_down(q):
-        peer = jnp.maximum(row - 1, 0)
-        return copy_to("row", peer, mirror.at[q], high.at[q], chain_send.at[q], high_recv.at[q])
-
-    def hop(q, go, act):
-        pl.when(go & (row < root))(lambda: act(hop_up(q)))
-        pl.when(go & (row > root))(lambda: act(hop_down(q)))
-
-    for q in range(PARTS):
-        hop(q, is_end, lambda copy: copy.start())
-
-    terms = dot3(out_c[...], jnp.where(global_row >= global_col, matrix, 0.0), NT)
-    acc[...] = terms.reshape(acc.shape)
-    started = []
-
-    def chunk_of(q):
-        return q * halves // PARTS, (q * per) % count
-
-    for q in range(PARTS):
-
-        @pl.when(from_low)
-        def _():
-            copy_to(
-                "row", jnp.maximum(row - 1, 0), mirror.at[q], low.at[q], chain_send.at[q],
-                low_recv.at[q],
-            ).wait_recv()
-            mirror[q] += low[q]
-
-        @pl.when(from_high)
-        def _():
-            copy_to(
-                "row", jnp.minimum(row + 1, row_count - 1), mirror.at[q], high.at[q],
-                chain_send.at[q], high_recv.at[q],
-            ).wait_recv()
-            mirror[q] += high[q]
-
-        hop(q, jnp.logical_not(is_end), lambda copy: copy.start())
-        h, first = chunk_of(q)
-
-        @pl.when(row == root)
-        def _():
-            for k in range(tile_cols):
-                where = pl.ds(pl.multiple_of((k * groups + slot) * tile, tile), tile)
-                value = mirror[q, :, k * tile : (k + 1) * tile].reshape(per, sub, tile)
-                acc[h, first : first + per, :, where] += value
-
-        if (q + 1) % (PARTS // halves) == 0:
-            for k in range(half):
-                j = 2 * k + 1 - parity
-                started.append(
-                    copy_to("col", sibling, acc.at[h, j], near.at[h, k], nsend.at[h, k], nrecv.at[h, k])
-                )
-                started[-1].start()
-
     block = dot(inv, top[...], NN) + unit(tile)
     factor = factor_steps(dot(block, block, TN), work)
 
@@ -418,6 +421,7 @@
                 )
             )
             started[-1].start()
+    out_c[...] = dot3(inv, panel_c[...], NN)
     next(factor, None)
 
     gathers = [
@@ -491,13 +495,13 @@
         [pieces[:, h * sub : (h + 1) * sub].reshape(tile // halves, tile) for h in range(halves)],
         axis=0,
     )
-    mixed = -0.5 * dot(dot(reflect, curvature_t, TN), reflect, NN)
-    update_r[...] = dot3(reflect, full[...].reshape(tile, width), TN) + dot3(mixed, vectors, NN)
-    update_c[...] = dot3(reflect, picked[...].reshape(tile, -1), TN) + dot3(mixed, out_c[...], NN)
+    both = dot(reflect, inv, TN)
+    mixed = -0.5 * dot(dot(both, curvature_t, NN), reflect, NN)
+    update_r[...] = dot3(both, full[...].reshape(tile, width), NN) + dot3(mixed, vectors, NN)
+    update_c[...] = dot3(both, picked[...].reshape(tile, -1), NN) + dot3(mixed, out_c[...], NN)
     out_mine[...] = out_r[pl.ds(pl.multiple_of(col * span, span), span), :]
 
     for q in range(PARTS):
-        hop(q, row != root, lambda copy: copy.wait_send())
         pass_on(q, row >= 0, lambda copy: copy.wait_send())
     curve_sum.drain()
     for each in (*gathers, curve_gather):
@@ -519,7 +523,7 @@
     return matrix, global_row, global_col
 
 
-def product_step(lines, panel_r, panel_c, top, inverse, row_count, count, groups, tile_cols):
+def product_step(lines, panel_r, panel_c, top, inverse, mirror, row_count, count, groups, tile_cols):
     tile, width = panel_r.shape
     cols = panel_c.shape[1]
     span, half = tile // count, count // 2
@@ -536,12 +540,9 @@
             shape(tile, tile),
             shape(span, width),
         ],
-        in_specs=in_vmem(5),
+        in_specs=in_vmem(6),
         out_specs=in_vmem(6),
         scratch_shapes=[
-            VMEM(part, F32),
-            VMEM(part, F32),
-            VMEM(part, F32),
             VMEM((halves, count, sub, width), F32),
             VMEM((halves, half, sub, width), F32),
             VMEM((halves, half, sub, width), F32),
@@ -554,9 +555,6 @@
             VMEM((span, tile), F32),
             VMEM((count, span, tile), F32),
             VMEM((tile, 2 * tile), F32),
-            DMA((PARTS,)),
-            DMA((PARTS,)),
-            DMA((PARTS,)),
             DMA((halves, half)),
             DMA((halves, half)),
             DMA((halves, half)),
@@ -569,10 +567,13 @@
             *gather_sems(count),
         ],
         compiler_params=params(1),
-    )(lines, panel_r, panel_c, top, inverse)
-
-
-def update_kernel(row_count, count, tile_cols, where, lines, yr, xr, yc, xc, out):
+    )(lines, panel_r, panel_c, top, inverse, mirror)
+
+
+def update_kernel(
+    row_count, count, tile_cols,
+    where, lines, yr, xr, yc, xc, band, reflector, mine, out, out_band, out_reflector, out_mine,
+):
     tile = yr.shape[0]
     strips = tile_cols * tile // 128
     step = pl.program_id(0)
@@ -588,22 +589,39 @@
         value = lines[rows, :] - correction[:, k * 128 : (k + 1) * 128]
         out[rows, :] = jnp.where(global_row >= first + c, value, 0.0)
 
-
-def update_step(where, lines, yr, xr, yc, xc, row_count, count, tile_cols):
+    @pl.when(step == 0)
+    def _():
+        out_band[...] = band[...]
+        out_reflector[...] = reflector[...]
+        span, width = mine.shape
+        for k in range(width // 128):
+            rows = pl.ds(k, span, stride=width // 128)
+            out_mine[rows, :] = mine[:, k * 128 : (k + 1) * 128]
+
+
+def update_step(where, lines, yr, xr, yc, xc, rest, row_count, count, tile_cols):
     tile, width = yr.shape
     steps = width // tile
     block = (lines.shape[0] // steps, 128)
     strip = pl.BlockSpec((tile, tile), lambda i: (0, i))
-    whole = pl.BlockSpec(yc.shape, lambda i: (0, 0))
+    band, reflector, mine = rest
+    mine_lines = shape(mine.size // 128, 128)
+
+    def whole(array):
+        return pl.BlockSpec(array.shape, lambda i: (0, 0))
+
     lined = pl.BlockSpec(block, lambda i: (i, 0))
     return pl.pallas_call(
         functools.partial(update_kernel, row_count, count, tile_cols),
         grid=(steps,),
-        out_shape=shape(*lines.shape),
-        in_specs=[pl.BlockSpec(memory_space=pltpu.SMEM), lined, strip, strip, whole, whole],
-        out_specs=lined,
+        out_shape=[shape(*lines.shape), shape(tile, tile), shape(tile, tile), mine_lines],
+        in_specs=[
+            pl.BlockSpec(memory_space=pltpu.SMEM), lined, strip, strip, whole(yc), whole(xc),
+            whole(band), whole(reflector), whole(mine),
+        ],
+        out_specs=[lined, whole(band), whole(reflector), whole(mine_lines)],
         compiler_params=params(),
-    )(where, lines, yr, xr, yc, xc)
+    )(where, lines, yr, xr, yc, xc, band, reflector, mine)
 
 
 def body(matrix, panel_t):
@@ -613,18 +631,23 @@
     span, width = tile // count, tile_rows * tile
     lines = matrix.reshape(-1, 128)
     sizes = (row_count, count, groups, tile_cols)
-    panel_r, panel_c, top, band_block, inverse = panel_step(panel_t.reshape(span, width), *sizes)
+    panel_r, panel_c, top, band, inverse, mirror = panel_step(
+        panel_t.reshape(-1, 128), lines, tile, *sizes
+    )
     yr, yc, xr, xc, reflector, vectors = product_step(
         lines,
         panel_r.reshape(tile, width),
         panel_c.reshape(tile, -1),
         top.reshape(tile, tile),
         inverse,
+        mirror,
         *sizes,
     )
     where = jnp.stack([lax.axis_index("row"), lax.axis_index("col")])
-    updated = update_step(where, lines, yr, xr, yc, xc, row_count, count, tile_cols)
-    return (updated.reshape(matrix.shape), vectors.reshape(panel_t.shape), band_block, reflector)
+    updated, band, reflector, vectors = update_step(
+        where, lines, yr, xr, yc, xc, (band, reflector, vectors), row_count, count, tile_cols
+    )
+    return (updated.reshape(matrix.shape), vectors.reshape(panel_t.shape), band, reflector)
 
 
 def solution(mesh):

time: 113 us -> 105 us (0.929)
  Pallas kernels: 109 us -> 102 us
  other arithmetic: 1.32 us -> 0.08 us
    pallas_call x1, Pallas kernels: 66.5 us -> 58.7 us  [product_step(): pl.pallas_call(functools.partial(product_kernel, row_count, count, groups...]
    unnamed x1 -> x0, other arithmetic: 1.25 us -> none
    unnamed x5 -> x6, local copies, waits for them, and re-layouts: 1.44 us -> 2.5 us
where the time goes in v3:
time: 105 us
  Pallas kernels  102 us (97%)
  local copies, waits for them, and re-layouts  2.5 us (2%)
    pallas_call x1, Pallas kernels, product_step(): pl.pallas_call(functools.partial(product_kernel, row_count, count, groups...  58.7 us
    pallas_call x1, Pallas kernels, panel_step(): pl.pallas_call(functools.partial(panel_kernel, row_count, count, groups,...  38.8 us
    pallas_call x1, Pallas kernels, update_step(): pl.pallas_call(functools.partial(update_kernel, row_count, count, tile_co...  4.39 us
    unnamed x6, local copies, waits for them, and re-layouts  2.5 us

profile of v3, /device:TPU:3, one launch (start us, length us, event | category | flops | bytes accessed | tf_op | source)
XLA Modules:
  0.0 105.1 jit_solution(4890965201099475851)
XLA Ops:
  0.6 0.1 pad_add_fusion.where
  0.7 0.0 copy-start
  0.7 1.6 %copy-done = f32[4,1,256,2,1,256]{5,4,3,2,1,0:T(1,128)S(1)} copy-done((f32[4,1,256,2,1,256]{5,4,3,2,1,0:T(1,128)S(1)}, f32[4,1,256,2,1,256]{5,4,3,2,1,0:T(1,128)}, u32[]{:S(2)}) %copy-start) | copy-done | bytes 2097176
  2.3 0.0 copy-start.2
  2.3 0.9 copy-done.2
  3.2 38.8 %shard_map.57 = (f32[8,32,1024]{2,1,0:T(8,128)S(1)}, f32[8,32,512]{2,1,0:T(8,128)S(1)}, f32[8,32,256]{2,1,0:T(8,128)S(1)}, f32[256,256]{1,0:T(8,128)S(1)}, f32[2...) custom-call(f32[256,128]{1,0:T(8,128)S(1)} %bitcast.15, f32[4096,128]{1,0:T(8,128)S(1)} %bitcast.10), custom_call_target="tpu_custom_call" | custom-call | tf_op jit(solution)/shard_map/pallas_call | solution.py:324
  42.0 0.0 copy-start.1
  42.0 58.7 %shard_map.58 = (f32[256,1024]{1,0:T(8,128)S(1)}, f32[256,512]{1,0:T(8,128)S(1)}, f32[256,1024]{1,0:T(8,128)S(1)}, f32[256,512]{1,0:T(8,128)S(1)}, f32[256,256]{1,0:T(8,128)S(1)}, /*index=5*/f32[32,1024]{1,0:T(8,128)S(1)}) custom-call(f32[4096,128]{1,0:T(8,128)} %bitcast.9, f32[256,1024]{1,0:T(8,128)S(1)} %bitcast.12, f32[256,512]{1,0:T(8,128)S(1)} %bitcast.13, ...), custom_call_target="tpu_custom_call" | custom-call | tf_op jit(solution)/shard_map/pallas_call | solution.py:533
  100.7 0.0 copy-done.1
  100.7 4.4 %shard_map.59 = (f32[4096,128]{1,0:T(8,128)}, f32[256,256]{1,0:T(8,128)}, f32[256,256]{1,0:T(8,128)}, f32[256,128]{1,0:T(8,128)}) custom-call(s32[2]{0:T(128)S(1)} %pad_add_fusion.where, f32[4096,128]{1,0:T(8,128)S(1)} %bitcast.11, f32[256,1024]{1,0:T(8,128)S(1)} %get-tuple-element.25.yr, f32[256,1024]{1,0:T(8,128)S(1)} %get-tuple-element.26.xr, ...), custom_call_target="tpu_custom_call" | custom-call | tf_op jit(solution)/shard_map/pallas_call | solution.py:614
Async XLA Ops:
  0.7 1.6 %copy-start = (f32[4,1,256,2,1,256]{5,4,3,2,1,0:T(1,128)S(1)}, f32[4,1,256,2,1,256]{5,4,3,2,1,0:T(1,128)}, u32[]{:S(2)}) copy-start(f32[4,1,256,2,1,256]{5,4,3,2,1,0:T(1,128)} %param.2) | copy-start | bytes 6291460
  2.3 0.9 copy-start.2
  42.0 58.7 %copy-start.1 = (f32[4,1,256,2,1,256]{5,4,3,2,1,0:T(1,128)S(1)}, f32[4,1,256,2,1,256]{5,4,3,2,1,0:T(1,128)}, u32[]{:S(2)}) copy-start(f32[4,1,256,2,1,256]{5,4,3,2,1,0:T(1,128)} %param.2) | copy-start | bytes 6291460

commit v4 on v3

--- a/solution.py
+++ b/solution.py
@@ -12,6 +12,7 @@
 HIGHEST = lax.Precision.HIGHEST
 BLOCK = 64
 GROUP = 4
+HOOK = 16
 
 
 def dot(a, b, over, precision=HIGHEST):
@@ -39,7 +40,7 @@
     return jax.ShapeDtypeStruct(dims, F32)
 
 
-def inverse_factor(block):
+def inverse_steps(block):
     size = block.shape[0]
     row = lax.broadcasted_iota(jnp.int32, (size, 2 * size), 0)
     col = lax.broadcasted_iota(jnp.int32, (size, 2 * size), 1)
@@ -47,6 +48,8 @@
     work = jnp.where(col == row + size, 1.0, work)
     scale = jnp.zeros((size, 2 * size), F32)
     for first in range(0, size, GROUP):
+        if first % HOOK == 0:
+            yield
         cols = [
             jnp.broadcast_to(work[:, first + t : first + t + 1], (size, 2 * size))
             for t in range(GROUP)
@@ -81,12 +84,11 @@
     work[:, size:] = unit(size)
     for lo in range(0, size, BLOCK):
         hi = lo + BLOCK
-        inv = inverse_factor(work[lo:hi, lo:hi])
+        inv = yield from inverse_steps(work[lo:hi, lo:hi])
         rows = dot(inv, work[lo:hi, :], NN)
         work[lo:hi, :] = rows
         if hi < size:
             work[hi:, :] -= dot(rows[:, hi:size], rows, TN)
-        yield
 
 
 def greet(row_peers, col_peers):
@@ -191,6 +193,38 @@
             self.copy(peer, self.me, k).wait_send()
 
 
+class RowRelay:
+    def __init__(self, src, slots, up, down, recv, count):
+        self.src, self.slots, self.sems, self.recv, self.count = src, slots, (up, down), recv, count
+        self.me = lax.axis_index("row")
+
+    def copy(self, slot, down):
+        peer = jnp.maximum(self.me - 1, 0) if down else jnp.minimum(self.me + 1, self.count - 1)
+        block = self.slots.at[slot]
+        return copy_to("row", peer, block, block, self.sems[down].at[slot], self.recv.at[slot])
+
+    def each(self, s, wait, act):
+        me, last = self.me, self.count - 1
+        for down in (0, 1):
+            here = me + s <= last if down else me >= s
+            there = me > 0 if down else me < last
+            slot = jnp.minimum(me + s, last) if down else jnp.maximum(me - s, 0)
+            if wait:
+                pl.when(here)(lambda: self.copy(slot, down).wait_recv())
+            pl.when(here & there)(lambda: act(self.copy(slot, down)))
+
+    def start(self):
+        self.slots[self.me] = self.src[...]
+        self.each(0, False, lambda copy: copy.start())
+
+    def step(self, s):
+        self.each(s, True, lambda copy: copy.start())
+
+    def drain(self):
+        for s in range(self.count):
+            self.each(s, False, lambda copy: copy.wait_send())
+
+
 DMA = pltpu.SemaphoreType.DMA
 
 
@@ -202,48 +236,91 @@
     return [DMA((count - 1,)), DMA((count,))]
 
 
+PARTS = 4
+
+
 def panel_kernel(
     row_count, count, groups, tile_cols,
-    own_lines, lines_hbm, panel_r, panel_c, top, band, inverse, mirror_sum,
-    mine, lines, mirror, from_rows, panel_z, part, slots, part_total, gram, work,
-    load, msend, mrecv, csend, crecv, *sems,
+    own_hbm, lines_hbm, panel_r, panel_c, top, band, inverse, mirror_sum,
+    mine, own_lines, lines, mirror, low, high, panel_z, part, slots, part_total, gram, work,
+    load, chain_send, low_recv, high_recv, csend, crecv, *sems,
 ):
     row, col = lax.axis_index("row"), lax.axis_index("col")
     span, width = mine.shape
     tile = span * count
     peers = others(col, count)
     root = lax.rem(col, row_count)
-    fetch = pltpu.make_async_copy(lines_hbm, lines, load)
+    own_fetch = pltpu.make_async_copy(own_hbm, own_lines, load.at[0])
+    own_fetch.start()
+    fetch = pltpu.make_async_copy(lines_hbm, lines, load.at[1])
     fetch.start()
+    greet(others(row, row_count), peers)
+    own_fetch.wait()
     strips = width // 128
     for k in range(strips):
         mine[:, k * 128 : (k + 1) * 128] = own_lines[pl.ds(k, span, stride=strips), :]
-    greet(others(row, row_count), peers)
     gather_r = Gather(mine, panel_r, sems[0:4], count)
     gather_g = Gather(part_total, gram, sems[4:8], count)
-    rows_z = RowSum(mine, panel_z, *sems[8:10], row_count)
-    rows_g = RowSum(part, slots, *sems[10:12], row_count)
+    rows_g = RowSum(part, slots, *sems[8:10], row_count)
+    rows_z = RowRelay(mine, panel_z, *sems[10:13], row_count)
     gather_r.start()
     rows_z.start()
     gather_r.finish()
     part[...] = dot(mine[...], panel_r[...].reshape(tile, -1), NT)
     rows_g.start()
+    rows_z.step(1)
     fetch.wait()
     matrix, global_row, global_col = read_matrix(lines, width, tile, row_count, count, tile_cols)
     strict = jnp.where(global_row > global_col, matrix, 0.0)
-    mirror[...] = dot3(panel_r[...].reshape(tile, width), strict, NN)
+    products = dot3(panel_r[...].reshape(tile, width), strict, NN)
+    mirror[...] = products.reshape(mirror.shape)
+    if row_count > 2:
+        rows_z.step(2)
     rows_g.finish()
     part_total[...] = rows_g.total()
     gather_g.start()
-    rows_z.finish()
+
+    depth = jnp.where(row > root, row_count - 1 - row, row)
+
+    def hop_up(q):
+        peer = jnp.minimum(row + 1, row_count - 1)
+        return copy_to("row", peer, mirror.at[q], low.at[q], chain_send.at[q], low_recv.at[q])
+
+    def hop_down(q):
+        peer = jnp.maximum(row - 1, 0)
+        return copy_to("row", peer, mirror.at[q], high.at[q], chain_send.at[q], high_recv.at[q])
+
+    def hop(q, act):
+        pl.when(row < root)(lambda: act(hop_up(q)))
+        pl.when(row > root)(lambda: act(hop_down(q)))
+
+    def take_low(q):
+        peer = jnp.maximum(row - 1, 0)
+        copy_to(
+            "row", peer, mirror.at[q], low.at[q], chain_send.at[q], low_recv.at[q]
+        ).wait_recv()
+        mirror[q] += low[q]
+
+    def take_high(q):
+        peer = jnp.minimum(row + 1, row_count - 1)
+        copy_to(
+            "row", peer, mirror.at[q], high.at[q], chain_send.at[q], high_recv.at[q]
+        ).wait_recv()
+        mirror[q] += high[q]
+
+    def relay(q):
+        pl.when(row < root)(lambda: take_low(q))
+        pl.when(row > root)(lambda: take_high(q))
+        hop(q, lambda copy: copy.start())
+
+    @pl.when((depth == 0) & (row != root))
+    def _():
+        for q in range(PARTS):
+            hop(q, lambda copy: copy.start())
+
+    for step in range(3, row_count):
+        rows_z.step(step)
     gather_g.finish()
-
-    place = jnp.maximum(lax.rem(row - root + row_count, row_count) - 1, 0)
-
-    def to_root():
-        return copy_to("row", root, mirror, from_rows.at[place], msend, mrecv.at[place])
-
-    pl.when(row != root)(lambda: to_root().start())
 
     def tiles_for(target):
         root, slot = lax.rem(target, row_count), target // row_count
@@ -269,8 +346,19 @@
         panel_c[col, :, at] = src[...]
     top[col] = panel_z[0, :, :tile]
 
-    for _ in factor_steps(gram[...].reshape(tile, tile), work):
-        pass
+    def relays(due):
+        for d in range(1, row_count - 1):
+            for q in range(PARTS):
+                if due(3 + 2 * q + 3 * (d - 1)):
+
+                    @pl.when((depth == d) & (row != root))
+                    def _():
+                        relay(q)
+
+    hooks = -1
+    for hooks, _ in enumerate(factor_steps(gram[...].reshape(tile, tile), work)):
+        relays(lambda at: at == hooks)
+    relays(lambda at: at > hooks)
     keep = lax.broadcasted_iota(jnp.int32, (tile, tile), 1) >= lax.broadcasted_iota(
         jnp.int32, (tile, tile), 0
     )
@@ -297,20 +385,11 @@
     def _():
         panel_c[:, :, :tile] += factor.reshape(count, span, tile)
 
-    @pl.when(row != root)
-    def _():
-        to_root().wait_send()
-        mirror_sum[...] = mirror[...]
-
-    @pl.when(row == root)
-    def _():
-        total = mirror[...]
-        for k in range(row_count - 1):
-            copy_to(
-                "row", lax.rem(root + k + 1, row_count), mirror, from_rows.at[k], msend, mrecv.at[k]
-            ).wait_recv()
-            total = total + from_rows[k]
-        mirror_sum[...] = total
+    for q in range(PARTS):
+        hop(q, lambda copy: copy.wait_send())
+        pl.when((row == root) & (row > 0))(lambda: take_low(q))
+        pl.when((row == root) & (row < row_count - 1))(lambda: take_high(q))
+    mirror_sum[...] = mirror[...].reshape(mirror_sum.shape)
 
     @pl.when((row == 0) & (col == 0))
     def _():
@@ -331,34 +410,36 @@
             shape(tile, tile),
             shape(tile, cols),
         ],
-        in_specs=in_vmem(1) + [pl.BlockSpec(memory_space=pl.ANY)],
+        in_specs=[pl.BlockSpec(memory_space=pltpu.HBM)] * 2,
         out_specs=in_vmem(6),
         scratch_shapes=[
             VMEM((span, width), F32),
+            VMEM(own_lines.shape, F32),
             VMEM(lines.shape, F32),
-            VMEM((tile, cols), F32),
-            VMEM((row_count - 1, tile, cols), F32),
+            VMEM((PARTS, tile // PARTS, cols), F32),
+            VMEM((PARTS, tile // PARTS, cols), F32),
+            VMEM((PARTS, tile // PARTS, cols), F32),
             VMEM((row_count, span, width), F32),
             VMEM((span, tile), F32),
             VMEM((row_count, span, tile), F32),
             VMEM((span, tile), F32),
             VMEM((count, span, tile), F32),
             VMEM((tile, 2 * tile), F32),
-            DMA,
-            DMA,
-            DMA((row_count - 1,)),
+            DMA((2,)),
+            DMA((PARTS,)),
+            DMA((PARTS,)),
+            DMA((PARTS,)),
             DMA((count - 1, tile_cols + 1)),
             DMA((count, tile_cols + 1)),
             *gather_sems(count),
             *gather_sems(count),
             *row_sems(row_count),
-            *row_sems(row_count),
+            DMA((row_count,)),
+            DMA((row_count,)),
+            DMA((row_count,)),
         ],
         compiler_params=params(0),
     )(own_lines, lines)
-
-
-PARTS = 4
 
 
 def product_kernel(
@@ -422,7 +503,8 @@
             )
             started[-1].start()
     out_c[...] = dot3(inv, panel_c[...], NN)
-    next(factor, None)
+    for _ in range(4):
+        next(factor, None)
 
     gathers = [
         Gather(summed.at[h], full.at[h], sems[4 * h : 4 * h + 4], count) for h in range(halves)
@@ -443,7 +525,6 @@
     curve_sum = RowSum(curve, slots, *sems[:2], row_count)
     curve_gather = Gather(curve_total, curvature, sems[2:6], count)
     curve_sum.start()
-    next(factor, None)
 
     def pass_up(q):
         peer = jnp.minimum(row + 1, row_count - 1)
@@ -477,16 +558,29 @@
             curve_sum.finish()
             curve_total[...] = curve_sum.total()
             curve_gather.start()
-    curve_gather.finish()
-    for q in range(PARTS):
+    away = jnp.where(row > root, row - root, root - row)
+    at_end = (row == 0) | (row == row_count - 1)
+
+    def arrive(q):
         pl.when(row > root)(lambda: pass_down(q).wait_recv())
         pl.when(row < root)(lambda: pass_up(q).wait_recv())
-        pass_on(q, row != root, lambda copy: copy.start())
-        if q in (0, PARTS - 1):
-            next(factor, None)
-    for _ in factor:
-        pass
-
+
+    def relays(due):
+        for d in range(1, row_count - 1):
+            for q in range(PARTS):
+                if due(2 * q + 2 * (d - 1)):
+
+                    @pl.when((away == d) & jnp.logical_not(at_end))
+                    def _():
+                        arrive(q)
+                        pass_on(q, row != root, lambda copy: copy.start())
+
+    hooks = -1
+    for hooks, _ in enumerate(factor):
+        relays(lambda at: at == hooks)
+        if hooks == 1:
+            curve_gather.finish()
+    relays(lambda at: at > hooks)
     inv2 = work[:, tile:]
     reflect = dot(inv2, dot(inv2, block, NT), TN)
     reflector[...] = reflect
@@ -498,6 +592,8 @@
     both = dot(reflect, inv, TN)
     mixed = -0.5 * dot(dot(both, curvature_t, NN), reflect, NN)
     update_r[...] = dot3(both, full[...].reshape(tile, width), NN) + dot3(mixed, vectors, NN)
+    for q in range(PARTS):
+        pl.when(at_end)(lambda: arrive(q))
     update_c[...] = dot3(both, picked[...].reshape(tile, -1), NN) + dot3(mixed, out_c[...], NN)
     out_mine[...] = out_r[pl.ds(pl.multiple_of(col * span, span), span), :]
 
@@ -527,7 +623,7 @@
     tile, width = panel_r.shape
     cols = panel_c.shape[1]
     span, half = tile // count, count // 2
-    halves = 2 if span % 16 == 0 else 1
+    halves = 4 if span % 32 == 0 else 1
     sub = span // halves
     part = (PARTS, tile // PARTS, cols)
     return pl.pallas_call(

time: 105 us -> 98.5 us (0.938); the launches traced: 105 us -> 97 us
  Pallas kernels: 102 us -> 93.8 us
    pallas_call x1, Pallas kernels: 58.7 us -> 46.6 us  [product_step(): pl.pallas_call(functools.partial(product_kernel, row_count, count, groups...]
    pallas_call x1, Pallas kernels: 38.8 us -> 42.8 us  [panel_step(): pl.pallas_call(functools.partial(panel_kernel, row_count, count, groups,...]
where the time goes in v4:
time: 98.5 us; the launch traced here: 97 us
  Pallas kernels  93.8 us (95%)
  local copies, waits for them, and re-layouts  2.5 us (3%)
    pallas_call x1, Pallas kernels, product_step(): pl.pallas_call(functools.partial(product_kernel, row_count, count, groups...  46.6 us
    pallas_call x1, Pallas kernels, panel_step(): pl.pallas_call(functools.partial(panel_kernel, row_count, count, groups,...  42.8 us
    pallas_call x1, Pallas kernels, update_step(): pl.pallas_call(functools.partial(update_kernel, row_count, count, tile_co...  4.39 us
    unnamed x6, local copies, waits for them, and re-layouts  2.5 us

profile of v4, /device:TPU:3, one launch (start us, length us, event | category | flops | bytes accessed | tf_op | source)
XLA Modules:
  0.0 97.0 jit_solution(4028005001777541518)
XLA Ops:
  0.6 0.1 pad_add_fusion.where
  0.7 0.0 copy-start
  0.7 1.6 %copy-done = f32[4,1,256,2,1,256]{5,4,3,2,1,0:T(1,128)S(1)} copy-done((f32[4,1,256,2,1,256]{5,4,3,2,1,0:T(1,128)S(1)}, f32[4,1,256,2,1,256]{5,4,3,2,1,0:T(1,128)}, u32[]{:S(2)}) %copy-start) | copy-done | bytes 2097176
  2.3 0.0 copy-start.2
  2.3 0.9 copy-done.2
  3.2 42.8 %shard_map.57 = (f32[8,32,1024]{2,1,0:T(8,128)S(1)}, f32[8,32,512]{2,1,0:T(8,128)S(1)}, f32[8,32,256]{2,1,0:T(8,128)S(1)}, f32[256,256]{1,0:T(8,128)S(1)}, f32[2...) custom-call(f32[256,128]{1,0:T(8,128)S(1)} %bitcast.15, f32[4096,128]{1,0:T(8,128)S(1)} %bitcast.10), custom_call_target="tpu_custom_call" | custom-call | tf_op jit(solution)/shard_map/pallas_call | solution.py:403
  46.0 0.0 copy-start.1
  46.0 46.6 %shard_map.58 = (f32[256,1024]{1,0:T(8,128)S(1)}, f32[256,512]{1,0:T(8,128)S(1)}, f32[256,1024]{1,0:T(8,128)S(1)}, f32[256,512]{1,0:T(8,128)S(1)}, f32[256,256]{1,0:T(8,128)S(1)}, /*index=5*/f32[32,1024]{1,0:T(8,128)S(1)}) custom-call(f32[4096,128]{1,0:T(8,128)} %bitcast.9, f32[256,1024]{1,0:T(8,128)S(1)} %bitcast.12, f32[256,512]{1,0:T(8,128)S(1)} %bitcast.13, ...), custom_call_target="tpu_custom_call" | custom-call | tf_op jit(solution)/shard_map/pallas_call | solution.py:629
  92.6 0.0 copy-done.1
  92.7 4.4 %shard_map.59 = (f32[4096,128]{1,0:T(8,128)}, f32[256,256]{1,0:T(8,128)}, f32[256,256]{1,0:T(8,128)}, f32[256,128]{1,0:T(8,128)}) custom-call(s32[2]{0:T(128)S(1)} %pad_add_fusion.where, f32[4096,128]{1,0:T(8,128)S(1)} %bitcast.11, f32[256,1024]{1,0:T(8,128)S(1)} %get-tuple-element.25.yr, f32[256,1024]{1,0:T(8,128)S(1)} %get-tuple-element.26.xr, ...), custom_call_target="tpu_custom_call" | custom-call | tf_op jit(solution)/shard_map/pallas_call | solution.py:710
Async XLA Ops:
  0.7 1.6 %copy-start = (f32[4,1,256,2,1,256]{5,4,3,2,1,0:T(1,128)S(1)}, f32[4,1,256,2,1,256]{5,4,3,2,1,0:T(1,128)}, u32[]{:S(2)}) copy-start(f32[4,1,256,2,1,256]{5,4,3,2,1,0:T(1,128)} %param.2) | copy-start | bytes 6291460
  2.3 0.9 copy-start.2
  46.0 46.6 %copy-start.1 = (f32[4,1,256,2,1,256]{5,4,3,2,1,0:T(1,128)S(1)}, f32[4,1,256,2,1,256]{5,4,3,2,1,0:T(1,128)}, u32[]{:S(2)}) copy-start(f32[4,1,256,2,1,256]{5,4,3,2,1,0:T(1,128)} %param.2) | copy-start | bytes 6291460

commit v5 on v4

--- a/solution.py
+++ b/solution.py
@@ -11,7 +11,7 @@
 VMEM = pltpu.VMEM
 HIGHEST = lax.Precision.HIGHEST
 BLOCK = 64
-GROUP = 4
+GROUP = 8
 HOOK = 16
 
 
@@ -42,28 +42,53 @@
 
 def inverse_steps(block):
     size = block.shape[0]
-    row = lax.broadcasted_iota(jnp.int32, (size, 2 * size), 0)
-    col = lax.broadcasted_iota(jnp.int32, (size, 2 * size), 1)
-    work = jnp.concatenate([block, jnp.zeros_like(block)], axis=1)
-    work = jnp.where(col == row + size, 1.0, work)
-    scale = jnp.zeros((size, 2 * size), F32)
-    for first in range(0, size, GROUP):
-        if first % HOOK == 0:
+    wide = (GROUP, 2 * size)
+    sub = lax.broadcasted_iota(jnp.int32, wide, 0)
+    lane = lax.broadcasted_iota(jnp.int32, wide, 1)
+    count = size // GROUP
+    work, scales = [], []
+    for g in range(count):
+        rows = block[g * GROUP : (g + 1) * GROUP, :]
+        rows = jnp.concatenate([rows, jnp.zeros_like(rows)], axis=1)
+        work.append(jnp.where(lane == sub + (g * GROUP + size), 1.0, rows))
+    for g in range(count):
+        if g * GROUP % HOOK == 0:
             yield
-        cols = [
-            jnp.broadcast_to(work[:, first + t : first + t + 1], (size, 2 * size))
-            for t in range(GROUP)
-        ]
+        first = g * GROUP
+        cols = {
+            r: [
+                jnp.broadcast_to(work[r][:, first + t : first + t + 1], wide)
+                for t in range(GROUP)
+            ]
+            for r in range(g, count)
+        }
+        pivot = [[cols[g][b][a : a + 1, :] for b in range(GROUP)] for a in range(GROUP)]
+        row = [work[g][a : a + 1, :] for a in range(GROUP)]
+        inverse = []
+        scale = jnp.zeros(wide, F32)
         for t in range(GROUP):
-            j = first + t
-            pivot = cols[t][j : j + 1, :]
-            guess = pl.reciprocal(pivot, approx=True)
-            factor = jnp.where(row > j, cols[t] * (guess * (2.0 - pivot * guess)), 0.0)
-            for u in range(t + 1, GROUP):
-                cols[u] = cols[u] - factor * cols[u][j : j + 1, :]
-            work = work - factor * work[j : j + 1, :]
-            scale = jnp.where(row == j, lax.rsqrt(pivot), scale)
-    return (work * scale)[:, size:]
+            guess = pl.reciprocal(pivot[t][t], approx=True)
+            inverse.append(guess * (2.0 - pivot[t][t] * guess))
+            scale = jnp.where(sub == t, lax.rsqrt(pivot[t][t]), scale)
+            for a in range(t + 1, GROUP):
+                factor = pivot[a][t] * inverse[t]
+                for b in range(t + 1, GROUP):
+                    pivot[a][b] = pivot[a][b] - factor * pivot[t][b]
+                row[a] = row[a] - factor * row[t]
+        scales.append(scale)
+        for r in range(g, count):
+            factors = []
+            for t in range(GROUP):
+                value = cols[r][t]
+                for s in range(t):
+                    value = value - factors[s] * pivot[s][t]
+                value = value * inverse[t]
+                factors.append(jnp.where(sub > t, value, 0.0) if r == g else value)
+            total = work[r]
+            for t in range(GROUP):
+                total = total - factors[t] * row[t]
+            work[r] = total
+    return jnp.concatenate([work[g] * scales[g] for g in range(count)], axis=0)[:, size:]
 
 
 def dot3(a, b, over):

time: 98.5 us -> 95.7 us (0.972); the launches traced: 97 us -> 95.5 us
  Pallas kernels: 93.8 us -> 92.3 us
    pallas_call x1, Pallas kernels: 42.8 us -> 39.8 us  [panel_step(): pl.pallas_call(functools.partial(panel_kernel, row_count, count, groups,...]
    pallas_call x1, Pallas kernels: 46.6 us -> 48.1 us  [product_step(): pl.pallas_call(functools.partial(product_kernel, row_count, count, groups...]
where the time goes in v5:
time: 95.7 us; the launch traced here: 95.5 us
  Pallas kernels  92.3 us (96%)
  local copies, waits for them, and re-layouts  2.5 us (3%)
    pallas_call x1, Pallas kernels, product_step(): pl.pallas_call(functools.partial(product_kernel, row_count, count, groups...  48.1 us
    pallas_call x1, Pallas kernels, panel_step(): pl.pallas_call(functools.partial(panel_kernel, row_count, count, groups,...  39.8 us
    pallas_call x1, Pallas kernels, update_step(): pl.pallas_call(functools.partial(update_kernel, row_count, count, tile_co...  4.39 us
    unnamed x6, local copies, waits for them, and re-layouts  2.5 us

profile of v5, /device:TPU:3, one launch (start us, length us, event | category | flops | bytes accessed | tf_op | source)
XLA Modules:
  0.0 95.5 jit_solution(7748972976994147076)
XLA Ops:
  0.6 0.1 pad_add_fusion.where
  0.7 0.0 copy-start
  0.7 1.6 %copy-done = f32[4,1,256,2,1,256]{5,4,3,2,1,0:T(1,128)S(1)} copy-done((f32[4,1,256,2,1,256]{5,4,3,2,1,0:T(1,128)S(1)}, f32[4,1,256,2,1,256]{5,4,3,2,1,0:T(1,128)}, u32[]{:S(2)}) %copy-start) | copy-done | bytes 2097176
  2.3 0.0 copy-start.2
  2.3 0.9 copy-done.2
  3.2 39.8 %shard_map.57 = (f32[8,32,1024]{2,1,0:T(8,128)S(1)}, f32[8,32,512]{2,1,0:T(8,128)S(1)}, f32[8,32,256]{2,1,0:T(8,128)S(1)}, f32[256,256]{1,0:T(8,128)S(1)}, f32[2...) custom-call(f32[256,128]{1,0:T(8,128)S(1)} %bitcast.15, f32[4096,128]{1,0:T(8,128)S(1)} %bitcast.10), custom_call_target="tpu_custom_call" | custom-call | tf_op jit(solution)/shard_map/pallas_call | solution.py:428
  43.0 0.0 copy-start.1
  43.0 48.1 %shard_map.58 = (f32[256,1024]{1,0:T(8,128)S(1)}, f32[256,512]{1,0:T(8,128)S(1)}, f32[256,1024]{1,0:T(8,128)S(1)}, f32[256,512]{1,0:T(8,128)S(1)}, f32[256,256]{1,0:T(8,128)S(1)}, /*index=5*/f32[32,1024]{1,0:T(8,128)S(1)}) custom-call(f32[4096,128]{1,0:T(8,128)} %bitcast.9, f32[256,1024]{1,0:T(8,128)S(1)} %bitcast.12, f32[256,512]{1,0:T(8,128)S(1)} %bitcast.13, ...), custom_call_target="tpu_custom_call" | custom-call | tf_op jit(solution)/shard_map/pallas_call | solution.py:654
  91.1 0.0 copy-done.1
  91.2 4.4 %shard_map.59 = (f32[4096,128]{1,0:T(8,128)}, f32[256,256]{1,0:T(8,128)}, f32[256,256]{1,0:T(8,128)}, f32[256,128]{1,0:T(8,128)}) custom-call(s32[2]{0:T(128)S(1)} %pad_add_fusion.where, f32[4096,128]{1,0:T(8,128)S(1)} %bitcast.11, f32[256,1024]{1,0:T(8,128)S(1)} %get-tuple-element.25.yr, f32[256,1024]{1,0:T(8,128)S(1)} %get-tuple-element.26.xr, ...), custom_call_target="tpu_custom_call" | custom-call | tf_op jit(solution)/shard_map/pallas_call | solution.py:735
Async XLA Ops:
  0.7 1.6 %copy-start = (f32[4,1,256,2,1,256]{5,4,3,2,1,0:T(1,128)S(1)}, f32[4,1,256,2,1,256]{5,4,3,2,1,0:T(1,128)}, u32[]{:S(2)}) copy-start(f32[4,1,256,2,1,256]{5,4,3,2,1,0:T(1,128)} %param.2) | copy-start | bytes 6291460
  2.3 0.9 copy-start.2
  43.0 48.1 %copy-start.1 = (f32[4,1,256,2,1,256]{5,4,3,2,1,0:T(1,128)S(1)}, f32[4,1,256,2,1,256]{5,4,3,2,1,0:T(1,128)}, u32[]{:S(2)}) copy-start(f32[4,1,256,2,1,256]{5,4,3,2,1,0:T(1,128)} %param.2) | copy-start | bytes 6291460
